TPU v7x, 256 devices: a whole 4x4x8 slice. The times are simulated.
256 devices in a mesh: row: 16 (over y, z_hi), col: 16 (over x, z_lo, core).
Axes of the slice: x: 4, y: 4, z: 8 (z_hi: 4, z_lo: 2; z = z_hi * 2 + z_lo), core: 2. Of those that a mesh axis runs over, the one named last changes fastest.
Arguments:
- object_tiles: float32 [2, 2, 6144, 6144], P(None, None, 'row', 'col'), may hold values from -4 to 4
- probe_field: float32 [2, 128, 128], replicated, may hold values from -4 to 4
- prop_phase: float32 [128, 128], replicated, may hold values from -3.140625 to 3.140625
- intensity: float32 [2048, 128, 128], P(('row', 'col')), may hold values from 0 to 2
- positions: int32 [2048, 2], P(('row', 'col')), may hold values from 0 to 383
- counts: int32 [16, 16], P('row'), may hold values from 1 to 8, as said below
Outputs:
- object_new: float32 [2, 2, 6144, 6144], P(None, None, 'row', 'col')
Inputs may be any that keep to these rules, and one draw needn't show every extreme that they name: `counts`: in each row of the tile grid, in every aligned group of four tile columns 4j to 4j + 3, exactly two entries equal 8, and they sit at columns 4j and 4j + 1, or 4j + 2 and 4j + 3, or 4j and 4j + 2, or 4j + 1 and 4j + 3; the other two lie between 1 and 4.
All inputs are finite; a program needn't handle non-finite values.
Results may differ from a plain program's by a relative error of at most 0.0003.
Values sent between devices are 32-bit elements; how exact they have to be, the bound alone decides.
No kernel may reach another device: no remote copies, remote signals or barrier semaphores. Data moves between devices by JAX's collectives and lax.ppermute only.
A program may use at most 64 MiB of HBM per device.

v0:
```python
import functools

import numpy as np
import jax
import jax.numpy as jnp
from jax import lax
from jax.experimental import pallas as pl
from jax.experimental.pallas import tpu as pltpu
from jax.sharding import PartitionSpec as P
import ml_dtypes

ITERS = 2
STEP = 0.2
B = 128


def dft_tables():
    k = np.arange(B)
    phase = (np.outer(k, k) % B) * (2.0 * np.pi / B)
    c, s = np.cos(phase) / np.sqrt(B), -np.sin(phase) / np.sqrt(B)
    forward = np.block([[c, s], [-s, c]]).astype(np.float32)
    parts = []
    for full in (forward, forward.T):
        high = full.astype(ml_dtypes.bfloat16)
        low = (full - high.astype(np.float32)).astype(ml_dtypes.bfloat16)
        parts += [high, low]
    return np.stack(parts)


def split(x):
    high = x.astype(jnp.bfloat16)
    low = (x - high.astype(jnp.float32)).astype(jnp.bfloat16)
    return high, low


def dot(a, b):
    return jnp.dot(a, b, preferred_element_type=jnp.float32)


def right_mul(x, tab, at):
    high, low = split(x)
    t_high, t_low = tab[at], tab[at + 1]
    return dot(high, t_high) + (dot(low, t_high) + dot(high, t_low))


def left_mul(x, tab, at):
    high, low = split(x)
    t_high, t_low = tab[at], tab[at + 1]
    return dot(t_high, high) + (dot(t_high, low) + dot(t_low, high))


def rows_to_cols(y):
    top = jnp.concatenate([y[:B, :B], y[B:, :B]], axis=1)
    bottom = jnp.concatenate([y[:B, B:], y[B:, B:]], axis=1)
    return jnp.concatenate([top, bottom], axis=0)


def transform(re, im, tab, inverse):
    first, second = (2, 0) if inverse else (0, 2)
    x = jnp.concatenate(
        [jnp.concatenate([re[0], im[0]], axis=1), jnp.concatenate([re[1], im[1]], axis=1)], axis=0
    )
    y = rows_to_cols(right_mul(x, tab, first))
    z = left_mul(y, tab, second)
    return [z[:B, :B], z[:B, B:]], [z[B:, :B], z[B:, B:]]


PIECES = (
    ("core", ((1, 1), (1, 2), (2, 1), (2, 2))),
    ("top", ((0, 1), (0, 2))),
    ("left", ((1, 0), (2, 0))),
    ("first", ((0, 0),)),
    ("side", ((1, 3), (2, 3))),
    ("bottom", ((3, 1), (3, 2))),
    ("low", ((3, 0),)),
    ("ends", ((0, 3), (3, 3))),
)


def frames_kernel(last, pos_ref, cnt_ref, *refs):
    pieces, refs = refs[: len(PIECES)], refs[len(PIECES) :]
    inten_ref, probe_ref, kern_ref, tab = refs[:4]
    outs, (ext, grad, sems) = refs[4:-3], refs[-3:]
    copies = []
    for ref, (_, places) in zip(pieces, PIECES):
        for number, (rb, cb) in enumerate(places):
            copies.append(pltpu.make_async_copy(ref.at[number], ext.at[rb, cb], sems.at[rb * 4 + cb]))
    for c in copies:
        c.start()
    grad[...] = jnp.zeros_like(grad)
    for c in copies:
        c.wait()
    rows = lax.broadcasted_iota(jnp.int32, (B, B), 0)
    cols = lax.broadcasted_iota(jnp.int32, (B, B), 1)
    count = cnt_ref[0]

    def where_is(f):
        t, l = pos_ref[f, 0], pos_ref[f, 1]
        return t // B, lax.rem(t, B), l // B, lax.rem(l, B)

    def window(f):
        tb, ts, lb, ls = where_is(f)
        rm, cm = rows >= ts, cols >= ls

        def plane(k):
            upper = jnp.where(cm, ext[tb, lb, k], ext[tb, lb + 1, k])
            lower = jnp.where(cm, ext[tb + 1, lb, k], ext[tb + 1, lb + 1, k])
            return jnp.where(rm, upper, lower)

        return plane

    def probe(f):
        tb, ts, lb, ls = where_is(f)
        return [pltpu.roll(pltpu.roll(probe_ref[k], ts, 0), ls, 1) for k in range(2)]

    def add_back(f, planes):
        tb, ts, lb, ls = where_is(f)
        rm, cm = rows >= ts, cols >= ls
        zero = jnp.zeros((B, B), jnp.float32)
        for k, g in enumerate(planes):
            upper = jnp.where(rm, g, zero)
            lower = g - upper
            for db, part in ((0, upper), (1, lower)):
                left = jnp.where(cm, part, zero)
                grad[tb + db, lb, k] += left
                grad[tb + db, lb + 1, k] += part - left

    def pair(p, carry):
        fs = [2 * p, 2 * p + 1]
        win = [window(f) for f in fs]
        pr = [probe(f) for f in fs]
        o1r, o1i = [w(0) for w in win], [w(1) for w in win]
        ar = [pr[j][0] * o1r[j] - pr[j][1] * o1i[j] for j in range(2)]
        ai = [pr[j][0] * o1i[j] + pr[j][1] * o1r[j] for j in range(2)]
        fr, fi = transform(ar, ai, tab, False)
        kr, ki = kern_ref[0], kern_ref[1]
        mr = [kr * fr[j] - ki * fi[j] for j in range(2)]
        mi = [kr * fi[j] + ki * fr[j] for j in range(2)]
        br, bi = transform(mr, mi, tab, True)
        o2r, o2i = [w(2) for w in win], [w(3) for w in win]
        er = [br[j] * o2r[j] - bi[j] * o2i[j] for j in range(2)]
        ei = [br[j] * o2i[j] + bi[j] * o2r[j] for j in range(2)]
        pr_, pi_ = transform(er, ei, tab, False)
        mis = [pr_[j] * pr_[j] + pi_[j] * pi_[j] - inten_ref[fs[j]] for j in range(2)]
        gr, gi = transform([mis[j] * pr_[j] for j in range(2)], [mis[j] * pi_[j] for j in range(2)], tab, True)
        g2r = [br[j] * gr[j] + bi[j] * gi[j] for j in range(2)]
        g2i = [br[j] * gi[j] - bi[j] * gr[j] for j in range(2)]
        cr = [o2r[j] * gr[j] + o2i[j] * gi[j] for j in range(2)]
        ci = [o2r[j] * gi[j] - o2i[j] * gr[j] for j in range(2)]
        fr, fi = transform(cr, ci, tab, False)
        ur = [kr * fr[j] + ki * fi[j] for j in range(2)]
        ui = [kr * fi[j] - ki * fr[j] for j in range(2)]
        nr, ni = transform(ur, ui, tab, True)
        for j in range(2):
            g1r = pr[j][0] * nr[j] + pr[j][1] * ni[j]
            g1i = pr[j][0] * ni[j] - pr[j][1] * nr[j]

            @pl.when(fs[j] < count)
            def _():
                add_back(fs[j], [g1r, g1i, g2r[j], g2i[j]])
        return carry

    lax.fori_loop(0, (count + 1) // 2, pair, 0)


    if not last:
        copy = pltpu.make_async_copy(grad, outs[0], sems.at[0])
        copy.start()
        copy.wait()
    else:
        out_ref, right_ref, bottom_ref = outs
        copies = [
            pltpu.make_async_copy(grad.at[:, 3], right_ref, sems.at[9]),
            pltpu.make_async_copy(grad.at[3, pl.ds(0, 3)], bottom_ref, sems.at[10]),
        ]
        for c in copies:
            c.start()
        for rb in range(3):
            for cb in range(3):
                ext[rb, cb] = ext[rb, cb] - STEP * grad[rb, cb]
                c = pltpu.make_async_copy(
                    ext.at[rb, cb], out_ref.at[:, pl.ds(rb * B, B), pl.ds(cb * B, B)], sems.at[rb * 3 + cb]
                )
                c.start()
                copies.append(c)
        for c in copies:
            c.wait()


def frame_grads(last, positions, count, pieces, intensity, probe_field, kern, tab):
    anyspec = pl.BlockSpec(memory_space=pl.ANY)
    vmem = pl.BlockSpec(memory_space=pltpu.VMEM)
    smem = pl.BlockSpec(memory_space=pltpu.SMEM)
    shape = lambda *dims: jax.ShapeDtypeStruct(dims, jnp.float32)
    outs = [shape(4, 3 * B, 3 * B), shape(4, 4, B, B), shape(3, 4, B, B)] if last else [shape(4, 4, 4, B, B)]
    return pl.pallas_call(
        functools.partial(frames_kernel, last),
        out_shape=outs,
        in_specs=[smem, smem] + [anyspec] * len(PIECES) + [vmem] * 4,
        out_specs=[anyspec] * len(outs),
        scratch_shapes=[
            pltpu.VMEM((4, 4, 4, B, B), jnp.float32),
            pltpu.VMEM((4, 4, 4, B, B), jnp.float32),
            pltpu.SemaphoreType.DMA((16,)),
        ],
        compiler_params=pltpu.CompilerParams(vmem_limit_bytes=32 * 1024 * 1024),
        cost_estimate=pl.CostEstimate(flops=2 * 10**9, bytes_accessed=9 * 10**6, transcendentals=0),
        name="last_frames" if last else "frames",
    )(positions, count, *pieces, intensity, probe_field, kern, tab)


def passed_along(x, axis, by):
    count = lax.axis_size(axis)
    pairs = [(i, i + by) for i in range(count) if 0 <= i + by < count]
    return lax.ppermute(x, axis, pairs)


def local(object_tiles, probe_field, prop_phase, intensity, positions, counts):
    tile = object_tiles.reshape(4, 3 * B, 3 * B)

    def block(rb, cb):
        return tile[:, rb * B : (rb + 1) * B, cb * B : (cb + 1) * B]

    def blocks(places):
        return jnp.stack([block(*at) for at in places])

    places = dict(PIECES)
    count = counts[0, lax.axis_index("col")][None]
    inside = (lax.axis_index("row") < lax.axis_size("row") - 1).astype(jnp.float32)
    kern = jnp.stack([jnp.cos(prop_phase), jnp.sin(prop_phase)])
    tab = jnp.asarray(dft_tables())
    consts = (intensity, probe_field, kern, tab)

    first, top, left = blocks(places["first"]), blocks(places["top"]), blocks(places["left"])
    low = passed_along(first, "row", -1)
    bottom = passed_along(top, "row", -1)
    end_top = passed_along(first, "col", -1)
    side = passed_along(left, "col", -1)
    end_low = passed_along(low, "col", -1)
    core = blocks(places["core"])
    ends = jnp.concatenate([end_top, end_low])
    (grad,) = frame_grads(False, positions, count, (core, top, left, first, side, bottom, low, ends), *consts)

    cross = passed_along(jnp.stack([grad[0, 3], grad[3, 3]]), "col", 1)
    up = passed_along(grad[0, 1:3], "row", -1)
    down = passed_along(grad[3, 1:3], "row", 1)
    over = passed_along(grad[1:3, 3], "col", 1)
    corner_top, corner_low = grad[0, 0] + cross[0], grad[3, 0] + cross[1]
    up_first = passed_along(corner_top, "row", -1)
    down_first = passed_along(corner_low, "row", 1)
    g_left = grad[1:3, 0] + over
    g_side = passed_along(g_left, "col", -1)
    g_first = corner_top + down_first
    g_low = (corner_low + up_first) * inside
    g_ends = passed_along(jnp.stack([g_first, g_low]), "col", -1)

    core = core - STEP * grad[1:3, 1:3].reshape(core.shape)
    top = top - STEP * (grad[0, 1:3] + down)
    left = left - STEP * g_left
    first = first - STEP * g_first[None]
    side = side - STEP * g_side
    bottom = bottom - STEP * ((grad[3, 1:3] + up) * inside)
    low = low - STEP * g_low[None]
    ends = ends - STEP * g_ends
    out, right, under = frame_grads(True, positions, count, (core, top, left, first, side, bottom, low, ends), *consts)

    cross = passed_along(right[3], "col", 1)
    down = passed_along(under[1:3], "row", 1)
    over = passed_along(right[0:3], "col", 1)
    down_first = passed_along(under[0] + cross, "row", 1)
    top_add = jnp.concatenate([down_first, down[0], down[1]], axis=2)
    left_add = over.transpose(1, 0, 2, 3).reshape(4, 3 * B, B)
    out = out.at[:, :B, :].add(-STEP * top_add)
    out = out.at[:, :, :B].add(-STEP * left_add)
    return out.reshape(object_tiles.shape)


def solution(mesh):
    return jax.shard_map(
        local,
        mesh=mesh,
        in_specs=(
            P(None, None, "row", "col"),
            P(),
            P(),
            P(("row", "col"), None, None),
            P(("row", "col"), None),
            P("row", None),
        ),
        out_specs=P(None, None, "row", "col"),
        check_vma=False,
    )
```

profile of v0, /device:TPU:23, one launch (start us, length us, event | category | flops | bytes accessed | tf_op | source)
XLA Modules:
  0.0 213.2 jit_solution(6151188076720459358)
XLA Ops:
  0.0 2.7 %slice_bitcast_fusion.21 = (f32[1,4,128,128]{3,2,1,0:T(8,128)S(1)}, f32[1,4,128,128]{3,2,1,0:T(8,128)S(1)}, f32[1,4,128,128]{3,2,1,0:T(8,128)S(1)}, f32[1,4,128,...) fusion(f32[4,384,384]{2,1,0:T(8,128)} %bitcast.88), kind=kLoop, calls=%fused_computation.46 | loop fusion | bytes 4718592 | tf_op jit(solution)/shard_map/stack | solution.py:225
  2.8 7.9 %collective-permute-start.2 = (f32[1,4,128,128]{3,2,1,0:T(8,128)S(1)}, f32[1,4,128,128]{3,2,1,0:T(8,128)S(1)}, u32[]{:S(2)}, u32[]{:S(2)}) collective-permute-start(f32[1,4,128,128]{3,2,1,0:T(8,128)S(1)} %get-tuple-element.47.refs_3_), channel_id=1, source_target_pairs={{16,0},{32,16},{48,32},{64,48},{80,64},{96,80},{112,96},{128,112},... | collective-permute-start | bytes 786440 | tf_op jit(solution)/shard_map/ppermute | solution.py:215
  10.7 2.9 %collective-permute-start.3 = (f32[1,4,128,128]{3,2,1,0:T(8,128)S(1)}, f32[1,4,128,128]{3,2,1,0:T(8,128)}, u32[]{:S(2)}, u32[]{:S(2)}) collective-permute-start(f32[1,4,128,128]{3,2,1,0:T(8,128)S(1)} %get-tuple-element.47.refs_3_), channel_id=1, source_target_pairs={{1,0},{2,1},{3,2},{4,3},{5,4},{6,5},{7,6},{8,7},{9,8},{10,9},{11,1... | collective-permute-start | bytes 786440 | tf_op jit(solution)/shard_map/ppermute | solution.py:215
  13.7 2.5 %collective-permute-start = (f32[2,4,128,128]{3,2,1,0:T(8,128)S(1)}, f32[2,4,128,128]{3,2,1,0:T(8,128)S(1)}, u32[]{:S(2)}, u32[]{:S(2)}) collective-permute-start(f32[2,4,128,128]{3,2,1,0:T(8,128)S(1)} %pad_maximum_fusion.2.refs_2_), channel_id=1, source_target_pairs={{1,0},{2,1},{3,2},{4,3},{5,4},{6,5},{7,6},{8,7},{9,8},{10,9},{11,1... | collective-permute-start | bytes 1572872 | tf_op jit(solution)/shard_map/ppermute | solution.py:215
  16.3 3.1 %collective-permute-start.1 = (f32[2,4,128,128]{3,2,1,0:T(8,128)S(1)}, f32[2,4,128,128]{3,2,1,0:T(8,128)S(1)}, u32[]{:S(2)}, u32[]{:S(2)}) collective-permute-start(f32[2,4,128,128]{3,2,1,0:T(8,128)S(1)} %pad_maximum_fusion.1.refs_1_), channel_id=1, source_target_pairs={{16,0},{32,16},{48,32},{64,48},{80,64},{96,80},{112,96},{128,112},... | collective-permute-start | bytes 1572872 | tf_op jit(solution)/shard_map/ppermute | solution.py:215
  19.6 5.0 %collective-permute-start.4 = (f32[1,4,128,128]{3,2,1,0:T(8,128)S(1)}, f32[1,4,128,128]{3,2,1,0:T(8,128)}, u32[]{:S(2)}, u32[]{:S(2)}) collective-permute-start(f32[1,4,128,128]{3,2,1,0:T(8,128)S(1)} %collective-permute-done.2.refs_6_), channel_id=1, source_target_pairs={{1,0},{2,1},{3,2},{4,3},{5,4},{6,5},{7,6},{8,7},{9,8},{10,9},{11,1... | collective-permute-start | bytes 786440 | tf_op jit(solution)/shard_map/ppermute | solution.py:215
  25.3 1.3 pad_maximum_fusion.refs_0_
  26.6 13.1 %collective-permute-done.3 = f32[1,4,128,128]{3,2,1,0:T(8,128)} collective-permute-done((f32[1,4,128,128]{3,2,1,0:T(8,128)S(1)}, f32[1,4,128,128]{3,2,1,0:T(8,128)}, u32[]{:S(2)}, u32[]{:S(2)}) %collective-permute-start.3) | collective-permute-done | bytes 262176 | tf_op jit(solution)/shard_map/ppermute | solution.py:215
  40.7 21.0 %collective-permute-done.4 = f32[1,4,128,128]{3,2,1,0:T(8,128)} collective-permute-done((f32[1,4,128,128]{3,2,1,0:T(8,128)S(1)}, f32[1,4,128,128]{3,2,1,0:T(8,128)}, u32[]{:S(2)}, u32[]{:S(2)}) %collective-permute-start.4) | collective-permute-done | bytes 262176 | tf_op jit(solution)/shard_map/ppermute | solution.py:215
  62.7 19.1 %frames.1 = f32[4,4,4,128,128]{4,3,2,1,0:T(8,128)S(1)} custom-call(s32[8,2]{1,0:T(8,128)S(1)} %copy.15.pos_ref, s32[1]{0:T(128)} %bitcast.cnt_ref, f32[4,4,128,128]{3,2,1,0:T(8,128)S(1)} %pad_maximum_fusion.refs_0_, f32[2,4,128,128]{3,2,1,0:T(8,128)S(1)} %pad_maximum_fusion.1.refs_1_, f32[2,4,128,128]{3,2,1,0:T(8,128)S(1)} %pad_maximum_fusion.2.refs_2_, ...), custom_call_target="tpu_custom_call" | custom-call | flops 2000000000 | bytes 9000000 | tf_op jit(solution)/shard_map/frames/pallas_call | solution.py:196
  81.9 1.9 collective-permute-start.10
  83.8 4.3 %collective-permute-start.5 = (f32[2,4,128,128]{3,2,1,0:T(8,128)S(1)}, f32[2,4,128,128]{3,2,1,0:T(8,128)S(1)}, u32[]{:S(2)}, u32[]{:S(2)}) collective-permute-start(f32[2,4,128,128]{3,2,1,0:T(8,128)S(1)} %get-tuple-element.44), channel_id=1, source_target_pairs={{0,16},{16,32},{32,48},{48,64},{64,80},{80,96},{96,112},{112,128},... | collective-permute-start | bytes 1572872 | tf_op jit(solution)/shard_map/ppermute | solution.py:215
  88.2 2.1 collective-permute-start.7
  90.3 1.9 collective-permute-start.6
  92.3 15.1 %collective-permute-done.7 = f32[2,4,128,128]{3,2,1,0:T(8,128)S(1)} collective-permute-done((f32[2,4,128,128]{3,2,1,0:T(8,128)S(1)}, f32[2,4,128,128]{3,2,1,0:T(8,128)S(1)}, u32[]{:S(2)}, u32[]{:S(2)}) %collective-permute-start.7) | collective-permute-done | bytes 524320 | tf_op jit(solution)/shard_map/ppermute | solution.py:215
  107.5 5.6 %collective-permute-start.8 = (f32[4,128,128]{2,1,0:T(8,128)S(1)}, f32[4,128,128]{2,1,0:T(8,128)S(1)}, u32[]{:S(2)}, u32[]{:S(2)}) collective-permute-start(f32[4,128,128]{2,1,0:T(8,128)S(1)} %fusion.4), channel_id=1, source_target_pairs={{0,16},{16,32},{32,48},{48,64},{64,80},{80,96},{96,112},{112,128},... | collective-permute-start | bytes 786440 | tf_op jit(solution)/shard_map/ppermute | solution.py:215
  113.3 17.1 %collective-permute-done.8 = f32[4,128,128]{2,1,0:T(8,128)S(1)} collective-permute-done((f32[4,128,128]{2,1,0:T(8,128)S(1)}, f32[4,128,128]{2,1,0:T(8,128)S(1)}, u32[]{:S(2)}, u32[]{:S(2)}) %collective-permute-start.8) | collective-permute-done | bytes 262176 | tf_op jit(solution)/shard_map/ppermute | solution.py:215
  130.5 1.9 collective-permute-start.11
  132.9 1.9 collective-permute-start.9
  134.8 3.7 %collective-permute-done.11 = f32[4,128,128]{2,1,0:T(8,128)S(1)} collective-permute-done((f32[4,128,128]{2,1,0:T(8,128)S(1)}, f32[4,128,128]{2,1,0:T(8,128)S(1)}, u32[]{:S(2)}, u32[]{:S(2)}) %collective-permute-start.11) | collective-permute-done | bytes 262176 | tf_op jit(solution)/shard_map/ppermute | solution.py:215
  138.6 1.9 collective-permute-start.12
  140.6 1.0 subtract_bitcast_fusion.refs_3_
  141.6 2.5 %collective-permute-done.9 = f32[2,4,128,128]{3,2,1,0:T(8,128)S(1)} collective-permute-done((f32[2,4,128,128]{3,2,1,0:T(8,128)S(1)}, f32[2,4,128,128]{3,2,1,0:T(8,128)S(1)}, u32[]{:S(2)}, u32[]{:S(2)}) %collective-permute-start.9) | collective-permute-done | bytes 524320 | tf_op jit(solution)/shard_map/ppermute | solution.py:215
  144.2 5.5 %collective-permute-done.12 = f32[2,4,128,128]{3,2,1,0:T(8,128)S(1)} collective-permute-done((f32[2,4,128,128]{3,2,1,0:T(8,128)S(1)}, f32[2,4,128,128]{3,2,1,0:T(8,128)S(1)}, u32[]{:S(2)}, u32[]{:S(2)}) %collective-permute-start.12) | collective-permute-done | bytes 524320 | tf_op jit(solution)/shard_map/ppermute | solution.py:215
  149.8 20.3 %last_frames.1 = (f32[4,384,384]{2,1,0:T(8,128)}, f32[4,4,128,128]{3,2,1,0:T(8,128)S(1)}, f32[3,4,128,128]{3,2,1,0:T(8,128)S(1)}) custom-call(s32[8,2]{1,0:T(8,128)S(1)} %copy.15.pos_ref, s32[1]{0:T(128)} %bitcast.cnt_ref, f32[4,4,128,128]{3,2,1,0:T(8,128)S(1)} %bitcast_subtract_fusion.refs_0_, f32[2,4,128,128]{3,2,1,0:T(8,128)S(1)} %get-tuple-element.40.refs_1_, ...), custom_call_target="tpu_custom_call" | custom-call | flops 2000000000 | bytes 9000000 | tf_op jit(solution)/shard_map/last_frames/pallas_call | solution.py:196
  170.2 3.7 %collective-permute-start.15 = (f32[2,4,128,128]{3,2,1,0:T(8,128)S(1)}, f32[2,4,128,128]{3,2,1,0:T(8,128)S(1)}, u32[]{:S(2)}, u32[]{:S(2)}) collective-permute-start(f32[2,4,128,128]{3,2,1,0:T(8,128)S(1)} %slice.151), channel_id=1, source_target_pairs={{0,16},{16,32},{32,48},{48,64},{64,80},{80,96},{96,112},{112,128},... | collective-permute-start | bytes 1572872 | tf_op jit(solution)/shard_map/ppermute | solution.py:215
  173.9 1.9 collective-permute-start.13
  175.9 1.9 collective-permute-start.16
  177.8 10.5 %collective-permute-done.13 = f32[4,128,128]{2,1,0:T(8,128)S(1)} collective-permute-done((f32[4,128,128]{2,1,0:T(8,128)S(1)}, f32[4,128,128]{2,1,0:T(8,128)S(1)}, u32[]{:S(2)}, u32[]{:S(2)}) %collective-permute-start.13) | collective-permute-done | bytes 262176 | tf_op jit(solution)/shard_map/ppermute | solution.py:215
  188.4 9.0 %collective-permute-start.14 = (f32[4,128,128]{2,1,0:T(8,128)S(1)}, f32[4,128,128]{2,1,0:T(8,128)S(1)}, u32[]{:S(2)}, u32[]{:S(2)}) collective-permute-start(f32[4,128,128]{2,1,0:T(8,128)S(1)} %bitcast_add_fusion), channel_id=1, source_target_pairs={{0,16},{16,32},{32,48},{48,64},{64,80},{80,96},{96,112},{112,128},... | collective-permute-start | bytes 786440 | tf_op jit(solution)/shard_map/ppermute | solution.py:215
  197.4 13.8 %collective-permute-done.14 = f32[4,128,128]{2,1,0:T(8,128)S(1)} collective-permute-done((f32[4,128,128]{2,1,0:T(8,128)S(1)}, f32[4,128,128]{2,1,0:T(8,128)S(1)}, u32[]{:S(2)}, u32[]{:S(2)}) %collective-permute-start.14) | collective-permute-done | bytes 262176 | tf_op jit(solution)/shard_map/ppermute | solution.py:215
  211.8 1.4 copy-done.17
  (78 shorter events, 4.9 us)
Async XLA Ops:
  0.0 24.7 %copy-start = (s32[1,16]{1,0:T(1,128)S(1)}, s32[1,16]{1,0:T(1,128)}, u32[]{:S(2)}) copy-start(s32[1,16]{1,0:T(1,128)} %param.16) | copy-start | bytes 196
  0.0 19.3 %copy-start.18 = (f32[128,128]{1,0:T(8,128)S(1)}, f32[128,128]{1,0:T(8,128)}, u32[]{:S(2)}) copy-start(f32[128,128]{1,0:T(8,128)} %param.13) | copy-start | bytes 196612
  2.8 21.8 %copy-start.19 = (s32[8,2]{0,1:T(2,128)S(1)}, s32[8,2]{0,1:T(2,128)}, u32[]{:S(2)}) copy-start(s32[8,2]{0,1:T(2,128)} %param.15) | copy-start | bytes 196
  2.8 16.8 %collective-permute-start.2 = (f32[1,4,128,128]{3,2,1,0:T(8,128)S(1)}, f32[1,4,128,128]{3,2,1,0:T(8,128)S(1)}, u32[]{:S(2)}, u32[]{:S(2)}) collective-permute-start(f32[1,4,128,128]{3,2,1,0:T(8,128)S(1)} %get-tuple-element.47.refs_3_), channel_id=1, source_target_pairs={{16,0},{32,16},{48,32},{64,48},{80,64},{96,80},{112,96},{128,112},... | collective-permute-start | bytes 786440 | tf_op jit(solution)/shard_map/ppermute | solution.py:215
  10.7 29.0 %collective-permute-start.3 = (f32[1,4,128,128]{3,2,1,0:T(8,128)S(1)}, f32[1,4,128,128]{3,2,1,0:T(8,128)}, u32[]{:S(2)}, u32[]{:S(2)}) collective-permute-start(f32[1,4,128,128]{3,2,1,0:T(8,128)S(1)} %get-tuple-element.47.refs_3_), channel_id=1, source_target_pairs={{1,0},{2,1},{3,2},{4,3},{5,4},{6,5},{7,6},{8,7},{9,8},{10,9},{11,1... | collective-permute-start | bytes 786440 | tf_op jit(solution)/shard_map/ppermute | solution.py:215
  13.7 49.0 %copy-start.1 = (f32[8,128,128]{2,1,0:T(8,128)S(1)}, f32[8,128,128]{2,1,0:T(8,128)}, u32[]{:S(2)}) copy-start(f32[8,128,128]{2,1,0:T(8,128)} %refs_8_.3) | copy-start | bytes 1572868
  13.7 49.0 %copy-start.3 = (f32[2,128,128]{2,1,0:T(8,128)S(1)}, f32[2,128,128]{2,1,0:T(8,128)}, u32[]{:S(2)}) copy-start(f32[2,128,128]{2,1,0:T(8,128)} %refs_9_.3) | copy-start | bytes 393220
  13.7 48.9 %collective-permute-start = (f32[2,4,128,128]{3,2,1,0:T(8,128)S(1)}, f32[2,4,128,128]{3,2,1,0:T(8,128)S(1)}, u32[]{:S(2)}, u32[]{:S(2)}) collective-permute-start(f32[2,4,128,128]{3,2,1,0:T(8,128)S(1)} %pad_maximum_fusion.2.refs_2_), channel_id=1, source_target_pairs={{1,0},{2,1},{3,2},{4,3},{5,4},{6,5},{7,6},{8,7},{9,8},{10,9},{11,1... | collective-permute-start | bytes 1572872 | tf_op jit(solution)/shard_map/ppermute | solution.py:215
  16.3 46.4 %collective-permute-start.1 = (f32[2,4,128,128]{3,2,1,0:T(8,128)S(1)}, f32[2,4,128,128]{3,2,1,0:T(8,128)S(1)}, u32[]{:S(2)}, u32[]{:S(2)}) collective-permute-start(f32[2,4,128,128]{3,2,1,0:T(8,128)S(1)} %pad_maximum_fusion.1.refs_1_), channel_id=1, source_target_pairs={{16,0},{32,16},{48,32},{64,48},{80,64},{96,80},{112,96},{128,112},... | collective-permute-start | bytes 1572872 | tf_op jit(solution)/shard_map/ppermute | solution.py:215
  19.6 42.0 %collective-permute-start.4 = (f32[1,4,128,128]{3,2,1,0:T(8,128)S(1)}, f32[1,4,128,128]{3,2,1,0:T(8,128)}, u32[]{:S(2)}, u32[]{:S(2)}) collective-permute-start(f32[1,4,128,128]{3,2,1,0:T(8,128)S(1)} %collective-permute-done.2.refs_6_), channel_id=1, source_target_pairs={{1,0},{2,1},{3,2},{4,3},{5,4},{6,5},{7,6},{8,7},{9,8},{10,9},{11,1... | collective-permute-start | bytes 786440 | tf_op jit(solution)/shard_map/ppermute | solution.py:215
  24.7 38.0 %copy-start.2 = (bf16[4,256,256]{2,1,0:T(8,128)(2,1)S(1)}, bf16[4,256,256]{2,1,0:T(8,128)(2,1)}, u32[]{:S(2)}) copy-start(bf16[4,256,256]{2,1,0:T(8,128)(2,1)} %constant.73.clone.refs_11_) | copy-start | bytes 1572868
  81.9 50.5 %collective-permute-start.10 = (f32[2,4,128,128]{3,2,1,0:T(8,128)S(1)}, f32[2,4,128,128]{3,2,1,0:T(8,128)S(1)}, u32[]{:S(2)}, u32[]{:S(2)}) collective-permute-start(f32[2,4,128,128]{3,2,1,0:T(8,128)S(1)} %get-tuple-element.43), channel_id=1, source_target_pairs={{16,0},{32,16},{48,32},{64,48},{80,64},{96,80},{112,96},{128,112},... | collective-permute-start | bytes 1572872 | tf_op jit(solution)/shard_map/ppermute | solution.py:215
  83.8 48.6 %collective-permute-start.5 = (f32[2,4,128,128]{3,2,1,0:T(8,128)S(1)}, f32[2,4,128,128]{3,2,1,0:T(8,128)S(1)}, u32[]{:S(2)}, u32[]{:S(2)}) collective-permute-start(f32[2,4,128,128]{3,2,1,0:T(8,128)S(1)} %get-tuple-element.44), channel_id=1, source_target_pairs={{0,16},{16,32},{32,48},{48,64},{64,80},{80,96},{96,112},{112,128},... | collective-permute-start | bytes 1572872 | tf_op jit(solution)/shard_map/ppermute | solution.py:215
  88.1 25.1 %copy-start.12 = (f32[1,4,128,128]{3,2,1,0:T(8,128)S(1)}, f32[1,4,128,128]{3,2,1,0:T(8,128)}, u32[]{:S(2)}) copy-start(f32[1,4,128,128]{3,2,1,0:T(8,128)} %get-tuple-element.52) | copy-start | bytes 786436
  88.1 25.1 %copy-start.13 = (f32[1,4,128,128]{3,2,1,0:T(8,128)S(1)}, f32[1,4,128,128]{3,2,1,0:T(8,128)}, u32[]{:S(2)}) copy-start(f32[1,4,128,128]{3,2,1,0:T(8,128)} %get-tuple-element.53) | copy-start | bytes 786436
  88.1 25.1 %copy-start.14 = (f32[1,4,128,128]{3,2,1,0:T(8,128)S(1)}, f32[1,4,128,128]{3,2,1,0:T(8,128)}, u32[]{:S(2)}) copy-start(f32[1,4,128,128]{3,2,1,0:T(8,128)} %get-tuple-element.54) | copy-start | bytes 786436
  88.1 25.1 %copy-start.15 = (f32[1,4,128,128]{3,2,1,0:T(8,128)S(1)}, f32[1,4,128,128]{3,2,1,0:T(8,128)}, u32[]{:S(2)}) copy-start(f32[1,4,128,128]{3,2,1,0:T(8,128)} %get-tuple-element.55) | copy-start | bytes 786436
  88.2 19.3 %collective-permute-start.7 = (f32[2,4,128,128]{3,2,1,0:T(8,128)S(1)}, f32[2,4,128,128]{3,2,1,0:T(8,128)S(1)}, u32[]{:S(2)}, u32[]{:S(2)}) collective-permute-start(f32[2,4,128,128]{3,2,1,0:T(8,128)S(1)} %pad_maximum_fusion.3), channel_id=1, source_target_pairs={{0,1},{1,2},{2,3},{3,4},{4,5},{5,6},{6,7},{7,8},{8,9},{9,10},{10,1... | collective-permute-start | bytes 1572872 | tf_op jit(solution)/shard_map/ppermute | solution.py:215
  90.3 42.2 %collective-permute-start.6 = (f32[2,4,128,128]{3,2,1,0:T(8,128)S(1)}, f32[2,4,128,128]{3,2,1,0:T(8,128)S(1)}, u32[]{:S(2)}, u32[]{:S(2)}) collective-permute-start(f32[2,4,128,128]{3,2,1,0:T(8,128)S(1)} %slice_bitcast_fusion), channel_id=1, source_target_pairs={{0,1},{1,2},{2,3},{3,4},{4,5},{5,6},{6,7},{7,8},{8,9},{9,10},{10,1... | collective-permute-start | bytes 1572872 | tf_op jit(solution)/shard_map/ppermute | solution.py:215
  107.5 25.0 %copy-start.5 = (f32[1,4,128,128]{3,2,1,0:T(8,128)S(1)}, f32[1,4,128,128]{3,2,1,0:T(8,128)}, u32[]{:S(2)}) copy-start(f32[1,4,128,128]{3,2,1,0:T(8,128)} %copy-done.4) | copy-start | bytes 786436
  107.5 25.0 %copy-start.7 = (f32[1,4,128,128]{3,2,1,0:T(8,128)S(1)}, f32[1,4,128,128]{3,2,1,0:T(8,128)}, u32[]{:S(2)}) copy-start(f32[1,4,128,128]{3,2,1,0:T(8,128)} %copy-done.6) | copy-start | bytes 786436
  107.5 25.0 %copy-start.9 = (f32[1,4,128,128]{3,2,1,0:T(8,128)S(1)}, f32[1,4,128,128]{3,2,1,0:T(8,128)}, u32[]{:S(2)}) copy-start(f32[1,4,128,128]{3,2,1,0:T(8,128)} %copy-done.8) | copy-start | bytes 786436
  107.5 25.0 %copy-start.11 = (f32[1,4,128,128]{3,2,1,0:T(8,128)S(1)}, f32[1,4,128,128]{3,2,1,0:T(8,128)}, u32[]{:S(2)}) copy-start(f32[1,4,128,128]{3,2,1,0:T(8,128)} %copy-done.10) | copy-start | bytes 786436
  107.5 22.9 %collective-permute-start.8 = (f32[4,128,128]{2,1,0:T(8,128)S(1)}, f32[4,128,128]{2,1,0:T(8,128)S(1)}, u32[]{:S(2)}, u32[]{:S(2)}) collective-permute-start(f32[4,128,128]{2,1,0:T(8,128)S(1)} %fusion.4), channel_id=1, source_target_pairs={{0,16},{16,32},{32,48},{48,64},{64,80},{80,96},{96,112},{112,128},... | collective-permute-start | bytes 786440 | tf_op jit(solution)/shard_map/ppermute | solution.py:215
  130.5 8.1 %collective-permute-start.11 = (f32[4,128,128]{2,1,0:T(8,128)S(1)}, f32[4,128,128]{2,1,0:T(8,128)S(1)}, u32[]{:S(2)}, u32[]{:S(2)}) collective-permute-start(f32[4,128,128]{2,1,0:T(8,128)S(1)} %get-tuple-element.36), channel_id=1, source_target_pairs={{16,0},{32,16},{48,32},{64,48},{80,64},{96,80},{112,96},{128,112},... | collective-permute-start | bytes 786440 | tf_op jit(solution)/shard_map/ppermute | solution.py:215
  132.9 11.2 %collective-permute-start.9 = (f32[2,4,128,128]{3,2,1,0:T(8,128)S(1)}, f32[2,4,128,128]{3,2,1,0:T(8,128)S(1)}, u32[]{:S(2)}, u32[]{:S(2)}) collective-permute-start(f32[2,4,128,128]{3,2,1,0:T(8,128)S(1)} %get-tuple-element.42), channel_id=1, source_target_pairs={{1,0},{2,1},{3,2},{4,3},{5,4},{6,5},{7,6},{8,7},{9,8},{10,9},{11,1... | collective-permute-start | bytes 1572872 | tf_op jit(solution)/shard_map/ppermute | solution.py:215
  138.6 11.1 %collective-permute-start.12 = (f32[2,4,128,128]{3,2,1,0:T(8,128)S(1)}, f32[2,4,128,128]{3,2,1,0:T(8,128)S(1)}, u32[]{:S(2)}, u32[]{:S(2)}) collective-permute-start(f32[2,4,128,128]{3,2,1,0:T(8,128)S(1)} %pad_maximum_fusion.4), channel_id=1, source_target_pairs={{1,0},{2,1},{3,2},{4,3},{5,4},{6,5},{7,6},{8,7},{9,8},{10,9},{11,1... | collective-permute-start | bytes 1572872 | tf_op jit(solution)/shard_map/ppermute | solution.py:215
  170.1 41.2 %copy-start.16 = (f32[4,384,384]{2,1,0:T(8,128)S(1)}, f32[4,384,384]{2,1,0:T(8,128)}, u32[]{:S(2)}) copy-start(f32[4,384,384]{2,1,0:T(8,128)} %get-tuple-element.32) | copy-start | bytes 7077892
  170.2 27.2 %collective-permute-start.15 = (f32[2,4,128,128]{3,2,1,0:T(8,128)S(1)}, f32[2,4,128,128]{3,2,1,0:T(8,128)S(1)}, u32[]{:S(2)}, u32[]{:S(2)}) collective-permute-start(f32[2,4,128,128]{3,2,1,0:T(8,128)S(1)} %slice.151), channel_id=1, source_target_pairs={{0,16},{16,32},{32,48},{48,64},{64,80},{80,96},{96,112},{112,128},... | collective-permute-start | bytes 1572872 | tf_op jit(solution)/shard_map/ppermute | solution.py:215
  173.9 14.4 %collective-permute-start.13 = (f32[4,128,128]{2,1,0:T(8,128)S(1)}, f32[4,128,128]{2,1,0:T(8,128)S(1)}, u32[]{:S(2)}, u32[]{:S(2)}) collective-permute-start(f32[4,128,128]{2,1,0:T(8,128)S(1)} %slice_bitcast_fusion.20), channel_id=1, source_target_pairs={{0,1},{1,2},{2,3},{3,4},{4,5},{5,6},{6,7},{7,8},{8,9},{9,10},{10,1... | collective-permute-start | bytes 786440 | tf_op jit(solution)/shard_map/ppermute | solution.py:215
  175.9 35.6 %collective-permute-start.16 = (f32[3,4,128,128]{3,2,1,0:T(8,128)S(1)}, f32[3,4,128,128]{3,2,1,0:T(8,128)S(1)}, u32[]{:S(2)}, u32[]{:S(2)}) collective-permute-start(f32[3,4,128,128]{3,2,1,0:T(8,128)S(1)} %slice.155), channel_id=1, source_target_pairs={{0,1},{1,2},{2,3},{3,4},{4,5},{5,6},{6,7},{7,8},{8,9},{9,10},{10,1... | collective-permute-start | bytes 2359304 | tf_op jit(solution)/shard_map/ppermute | solution.py:215
  188.4 22.9 %collective-permute-start.14 = (f32[4,128,128]{2,1,0:T(8,128)S(1)}, f32[4,128,128]{2,1,0:T(8,128)S(1)}, u32[]{:S(2)}, u32[]{:S(2)}) collective-permute-start(f32[4,128,128]{2,1,0:T(8,128)S(1)} %bitcast_add_fusion), channel_id=1, source_target_pairs={{0,16},{16,32},{32,48},{48,64},{64,80},{80,96},{96,112},{112,128},... | collective-permute-start | bytes 786440 | tf_op jit(solution)/shard_map/ppermute | solution.py:215
  (5 other events, 50.0 us)
where the time goes:
time: 215 us; the launch traced here: 213 us
  waiting for transfers between devices  102 us (47%)
  starting transfers between devices  59.4 us (28%)
  Pallas kernels  39.4 us (18%)
  local copies, waits for them, and re-layouts  7.48 us (3%)
  other arithmetic  3.88 us (2%)
    ppermute x17, waiting for transfers between devices, passed_along(): return lax.ppermute(x, axis, pairs)  102 us
    ppermute x17, starting transfers between devices, passed_along(): return lax.ppermute(x, axis, pairs)  59.4 us
    pallas_call x2, Pallas kernels, frame_grads(): pl.pallas_call(functools.partial(frames_kernel, last), out_shape=outs, in...  39.4 us
  transfers between devices with their start and end apart: 17, of which 9 were waited for; matrix products, arithmetic and copies ran while one was open for 3% of the time, Pallas kernels for 0%

commit v1 on v0

v1 whole, which is shorter than its diff:
```python
import functools

import numpy as np
import jax
import jax.numpy as jnp
from jax import lax
from jax.experimental import pallas as pl
from jax.experimental.pallas import tpu as pltpu
from jax.sharding import PartitionSpec as P
import ml_dtypes

ITERS = 2
STEP = 0.2
B = 128
ROWS, RING = 16, 4
SHARE = 32
GROUP = 8


def dft_tables():
    k = np.arange(B)
    phase = (np.outer(k, k) % B) * (2.0 * np.pi / B)
    c, s = np.cos(phase) / np.sqrt(B), -np.sin(phase) / np.sqrt(B)
    forward = np.block([[c, s], [-s, c]]).astype(np.float32)
    parts = []
    for full in (forward, forward.T):
        high = full.astype(ml_dtypes.bfloat16)
        low = (full - high.astype(np.float32)).astype(ml_dtypes.bfloat16)
        parts += [high, low]
    return np.stack(parts)


def split(x):
    high = x.astype(jnp.bfloat16)
    low = (x - high.astype(jnp.float32)).astype(jnp.bfloat16)
    return high, low


def dot(a, b):
    return jnp.dot(a, b, preferred_element_type=jnp.float32)


def right_mul(x, tab, at):
    high, low = split(x)
    t_high, t_low = tab[at], tab[at + 1]
    return dot(high, t_high) + (dot(low, t_high) + dot(high, t_low))


def left_mul(x, tab, at):
    high, low = split(x)
    t_high, t_low = tab[at], tab[at + 1]
    return dot(t_high, high) + (dot(t_high, low) + dot(t_low, high))


def transform(re, im, tab, inverse):
    first, second = (2, 0) if inverse else (0, 2)
    count = len(re)
    x = jnp.concatenate([jnp.concatenate([r, i], axis=1) for r, i in zip(re, im)], axis=0)
    y = right_mul(x, tab, first)
    y = [y[j * B : (j + 1) * B] for j in range(count)]
    y = jnp.concatenate(
        [jnp.concatenate([v[:, :B] for v in y], axis=1), jnp.concatenate([v[:, B:] for v in y], axis=1)], axis=0
    )
    z = left_mul(y, tab, second)
    return [z[:B, j * B : (j + 1) * B] for j in range(count)], [z[B:, j * B : (j + 1) * B] for j in range(count)]


PIECES = (
    ("core", ((1, 1), (1, 2), (2, 1), (2, 2))),
    ("top", ((0, 1), (0, 2))),
    ("left", ((1, 0), (2, 0))),
    ("first", ((0, 0),)),
    ("side", ((1, 3), (2, 3))),
    ("bottom", ((3, 1), (3, 2))),
    ("low", ((3, 0),)),
    ("ends", ((0, 3), (3, 3))),
)


def whole_blocks(ext, tile, right, low, bottom, rest, corner):
    for rb in range(3):
        for cb in range(3):
            yield tile.at[:, pl.ds(rb * B, B), pl.ds(cb * B, B)], ext.at[rb, cb]
        yield right.at[:, pl.ds(rb * B, B), :], ext.at[rb, 3]
    yield low, ext.at[3, 0]
    for cb in (1, 2):
        cols = pl.ds((cb - 1) * B, B)
        yield bottom.at[:, :, cols], ext.at[3, cb, :, pl.ds(0, B - SHARE), :]
        yield rest.at[:, :, cols], ext.at[3, cb, :, pl.ds(B - SHARE, SHARE), :]
    yield corner, ext.at[3, 3]


def piece_blocks(ext, *pieces):
    for ref, (_, places) in zip(pieces, PIECES):
        for number, (rb, cb) in enumerate(places):
            yield ref.at[number], ext.at[rb, cb]


def frames_kernel(last, n_pieces, pos_ref, cnt_ref, *refs):
    pieces, refs = refs[:n_pieces], refs[n_pieces:]
    inten_from, probe_ref, kern_ref, tab_from = refs[:4]
    outs, (ext, grad, inten_ref, tab, sems, late_sem) = refs[4:-6], refs[-6:]
    late = pltpu.make_async_copy(inten_from, inten_ref, late_sem)
    copies = [pltpu.make_async_copy(tab_from, tab, sems.at[0])]
    for src, dst in (piece_blocks if last else whole_blocks)(ext, *pieces):
        copies.append(pltpu.make_async_copy(src, dst, sems.at[len(copies)]))
    for c in copies:
        c.start()
    late.start()
    grad[...] = jnp.zeros_like(grad)
    for c in copies:
        c.wait()
    rows = lax.broadcasted_iota(jnp.int32, (B, B), 0)
    cols = lax.broadcasted_iota(jnp.int32, (B, B), 1)
    count = cnt_ref[0]

    def where_is(f):
        t, l = pos_ref[f, 0], pos_ref[f, 1]
        return t // B, lax.rem(t, B), l // B, lax.rem(l, B)

    def window(f):
        tb, ts, lb, ls = where_is(f)
        rm, cm = rows >= ts, cols >= ls

        def plane(k):
            upper = jnp.where(cm, ext[tb, lb, k], ext[tb, lb + 1, k])
            lower = jnp.where(cm, ext[tb + 1, lb, k], ext[tb + 1, lb + 1, k])
            return jnp.where(rm, upper, lower)

        return plane

    def probe(f):
        tb, ts, lb, ls = where_is(f)
        return [pltpu.roll(pltpu.roll(probe_ref[k], ts, 0), ls, 1) for k in range(2)]

    def add_back(f, planes):
        tb, ts, lb, ls = where_is(f)
        rm, cm = rows >= ts, cols >= ls
        zero = jnp.zeros((B, B), jnp.float32)
        for k, g in enumerate(planes):
            upper = jnp.where(rm, g, zero)
            lower = g - upper
            for db, part in ((0, upper), (1, lower)):
                left = jnp.where(cm, part, zero)
                grad[tb + db, lb, k] += left
                grad[tb + db, lb + 1, k] += part - left

    def group(p, carry):
        fs = [GROUP * p + j for j in range(GROUP)]
        win = [window(f) for f in fs]
        pr = [probe(f) for f in fs]
        o1r, o1i = [w(0) for w in win], [w(1) for w in win]
        ar = [pr[j][0] * o1r[j] - pr[j][1] * o1i[j] for j in range(GROUP)]
        ai = [pr[j][0] * o1i[j] + pr[j][1] * o1r[j] for j in range(GROUP)]
        fr, fi = transform(ar, ai, tab, False)
        kr, ki = kern_ref[0], kern_ref[1]
        mr = [kr * fr[j] - ki * fi[j] for j in range(GROUP)]
        mi = [kr * fi[j] + ki * fr[j] for j in range(GROUP)]
        br, bi = transform(mr, mi, tab, True)
        o2r, o2i = [w(2) for w in win], [w(3) for w in win]
        er = [br[j] * o2r[j] - bi[j] * o2i[j] for j in range(GROUP)]
        ei = [br[j] * o2i[j] + bi[j] * o2r[j] for j in range(GROUP)]
        pr_, pi_ = transform(er, ei, tab, False)
        late.wait()
        mis = [pr_[j] * pr_[j] + pi_[j] * pi_[j] - inten_ref[fs[j]] for j in range(GROUP)]
        gr, gi = transform([mis[j] * pr_[j] for j in range(GROUP)], [mis[j] * pi_[j] for j in range(GROUP)], tab, True)
        g2r = [br[j] * gr[j] + bi[j] * gi[j] for j in range(GROUP)]
        g2i = [br[j] * gi[j] - bi[j] * gr[j] for j in range(GROUP)]
        cr = [o2r[j] * gr[j] + o2i[j] * gi[j] for j in range(GROUP)]
        ci = [o2r[j] * gi[j] - o2i[j] * gr[j] for j in range(GROUP)]
        fr, fi = transform(cr, ci, tab, False)
        ur = [kr * fr[j] + ki * fi[j] for j in range(GROUP)]
        ui = [kr * fi[j] - ki * fr[j] for j in range(GROUP)]
        nr, ni = transform(ur, ui, tab, True)
        for j in range(GROUP):
            g1r = pr[j][0] * nr[j] + pr[j][1] * ni[j]
            g1i = pr[j][0] * ni[j] - pr[j][1] * nr[j]

            @pl.when(fs[j] < count)
            def _():
                add_back(fs[j], [g1r, g1i, g2r[j], g2i[j]])
        return carry

    group(0, 0)


    if not last:
        copies = [pltpu.make_async_copy(grad, outs[0], sems.at[0])]
        copies[0].start()
        for rb in range(4):
            for cb in range(3):
                ext[rb, cb] = ext[rb, cb] - STEP * grad[rb, cb]
            c = pltpu.make_async_copy(ext.at[rb, pl.ds(0, 3)], outs[1].at[rb], sems.at[1 + rb])
            c.start()
            copies.append(c)
    else:
        out_ref, right_ref, bottom_ref = outs
        copies = [
            pltpu.make_async_copy(grad.at[:, 3], right_ref, sems.at[9]),
            pltpu.make_async_copy(grad.at[3, pl.ds(0, 3)], bottom_ref, sems.at[10]),
        ]
        for c in copies:
            c.start()
        for rb in range(3):
            for cb in range(3):
                ext[rb, cb] = ext[rb, cb] - STEP * grad[rb, cb]
                c = pltpu.make_async_copy(
                    ext.at[rb, cb], out_ref.at[:, pl.ds(rb * B, B), pl.ds(cb * B, B)], sems.at[rb * 3 + cb]
                )
                c.start()
                copies.append(c)
    for c in copies:
        c.wait()


def frame_grads(last, positions, count, pieces, intensity, probe_field, kern, tab):
    anyspec = pl.BlockSpec(memory_space=pl.ANY)
    vmem = pl.BlockSpec(memory_space=pltpu.VMEM)
    hbm = pl.BlockSpec(memory_space=pltpu.HBM)
    smem = pl.BlockSpec(memory_space=pltpu.SMEM)
    shape = lambda *dims: jax.ShapeDtypeStruct(dims, jnp.float32)
    if last:
        outs = [shape(4, 3 * B, 3 * B), shape(4, 4, B, B), shape(3, 4, B, B)]
    else:
        outs = [shape(4, 4, 4, B, B), shape(4, 3, 4, B, B)]
    return pl.pallas_call(
        functools.partial(frames_kernel, last, len(pieces)),
        out_shape=outs,
        in_specs=[smem, smem] + [anyspec if last else hbm] * len(pieces) + [hbm, vmem, vmem, hbm],
        out_specs=[anyspec] * len(outs),
        scratch_shapes=[
            pltpu.VMEM((4, 4, 4, B, B), jnp.float32),
            pltpu.VMEM((4, 4, 4, B, B), jnp.float32),
            pltpu.VMEM((8, B, B), jnp.float32),
            pltpu.VMEM((4, 2 * B, 2 * B), jnp.bfloat16),
            pltpu.SemaphoreType.DMA((24,)),
            pltpu.SemaphoreType.DMA,
        ],
        compiler_params=pltpu.CompilerParams(vmem_limit_bytes=(32 if last else 60) * 1024 * 1024),
        cost_estimate=pl.CostEstimate(flops=2 * 10**9, bytes_accessed=9 * 10**6, transcendentals=0),
        name="last_frames" if last else "frames",
    )(positions, count, *pieces, intensity, probe_field, kern, tab)


def passed_around(x, by):
    places = [(y, z) for y in range(ROWS // RING) for z in range(RING)]
    for step in range(RING - 1):
        pairs = []
        for y, z in places:
            z_to = (z - by) % RING
            y_to = y
            if step == RING - 2:
                start = (z + by * step) % RING
                y_to = y + (start + by) // RING
            if 0 <= y_to < ROWS // RING:
                pairs.append((y * RING + z, y_to * RING + z_to))
        x = lax.ppermute(x, "row", pairs)
    return x


def passed_along(x, axis, by):
    count = lax.axis_size(axis)
    pairs = [(i, i + by) for i in range(count) if 0 <= i + by < count]
    return lax.ppermute(x, axis, pairs)


def local(object_tiles, probe_field, prop_phase, intensity, positions, counts):
    tile = object_tiles.reshape(4, 3 * B, 3 * B)
    count = counts[0, lax.axis_index("col")][None]
    inside = (lax.axis_index("row") < lax.axis_size("row") - 1).astype(jnp.float32)
    kern = jnp.stack([jnp.cos(prop_phase), jnp.sin(prop_phase)])
    tab = jnp.asarray(dft_tables())
    consts = (intensity, probe_field, kern, tab)

    low = passed_along(tile[:, :B, :B], "row", -1)
    bottom = passed_along(tile[:, : B - SHARE, B:], "row", -1)
    rest = passed_around(tile[:, B - SHARE : B, B:], -1)
    right = passed_along(tile[:, :, :B], "col", -1)
    corner = passed_along(low, "col", -1)
    grad, moved = frame_grads(
        False, positions, count, (tile, right, low, bottom, rest, corner), *consts
    )

    cross = passed_along(jnp.stack([grad[0, 3], grad[3, 3]]), "col", 1)
    up = passed_along(grad[0, 1:3], "row", -1)
    down = passed_along(grad[3, 1:3], "row", 1)
    over = passed_along(grad[1:3, 3], "col", 1)
    up_first = passed_along(grad[0, 0] + cross[0], "row", -1)
    down_first = passed_along(grad[3, 0] + cross[1], "row", 1)
    left = moved[1:3, 0] - STEP * over
    side = passed_along(left, "col", -1)
    first = moved[0, 0] - STEP * (cross[0] + down_first)
    low = (moved[3, 0] - STEP * (cross[1] + up_first)) * inside
    ends = passed_along(jnp.stack([first, low]), "col", -1)
    core = moved[1:3, 1:3].reshape(4, 4, B, B)
    top = moved[0, 1:3] - STEP * down
    bottom = (moved[3, 1:3] - STEP * up) * inside
    pieces = (core, top, left, first[None], side, bottom, low[None], ends)
    out, right, under = frame_grads(True, positions, count, pieces, *consts)

    cross = passed_along(right[3], "col", 1)
    down = passed_along(under[1:3, :, : B - SHARE], "row", 1)
    rest = passed_around(under[1:3, :, B - SHARE :], 1)
    down = jnp.concatenate([down, rest], axis=2)
    over = passed_along(right[0:3], "col", 1)
    down_first = passed_along(under[0] + cross, "row", 1)
    top_add = jnp.concatenate([down_first, down[0], down[1]], axis=2)
    left_add = over.transpose(1, 0, 2, 3).reshape(4, 3 * B, B)
    out = out.at[:, :B, :].add(-STEP * top_add)
    out = out.at[:, :, :B].add(-STEP * left_add)
    return out.reshape(object_tiles.shape)


def solution(mesh):
    return jax.shard_map(
        local,
        mesh=mesh,
        in_specs=(
            P(None, None, "row", "col"),
            P(),
            P(),
            P(("row", "col"), None, None),
            P(("row", "col"), None),
            P("row", None),
        ),
        out_specs=P(None, None, "row", "col"),
        check_vma=False,
    )
```

time: 215 us -> 200 us (0.930)
  waiting for transfers between devices: 102 us -> 51.7 us
  starting transfers between devices: 59.4 us -> 93.3 us
  Pallas kernels: 39.4 us -> 32.4 us
  local copies, waits for them, and re-layouts: 7.48 us -> 12.6 us
    ppermute x17 -> x16, waiting for transfers between devices: 102 us -> 44.3 us  [passed_along(): return lax.ppermute(x, axis, pairs)]
    ppermute x0 -> x6, starting transfers between devices: none -> 20.7 us  [passed_around(): x = lax.ppermute(x, 'row', pairs)]
    ppermute x17 -> x16, starting transfers between devices: 59.4 us -> 72.6 us  [passed_along(): return lax.ppermute(x, axis, pairs)]
    ppermute x0 -> x6, waiting for transfers between devices: none -> 7.4 us  [passed_around(): x = lax.ppermute(x, 'row', pairs)]
    pallas_call x2, Pallas kernels: 39.4 us -> 32.4 us  [frame_grads(): pl.pallas_call(functools.partial(frames_kernel, last, len(pieces)), out_s...]
    slice x1 -> x7, local copies, waits for them, and re-layouts: 0.04 us -> 4.26 us  [the longest x1 1.22 us: local(): right = passed_along(tile[:, :, :B], 'col', -1)]
    another operation x1 -> x0, local copies, waits for them, and re-layouts: 2.75 us -> none  [blocks(): return jnp.stack([block(*at) for at in places])]
  transfers between devices with their start and end apart: 17 -> 22, of which waited for: 9 -> 10; matrix products, arithmetic and copies ran while one was open for 3% -> 6% of each run, Pallas kernels for 0% -> 0%
where the time goes in v1:
time: 200 us; the launch traced here: 196 us
  starting transfers between devices  93.3 us (47%)
  waiting for transfers between devices  51.7 us (26%)
  Pallas kernels  32.4 us (16%)
  local copies, waits for them, and re-layouts  12.6 us (6%)
  other arithmetic  5.72 us (3%)
    ppermute x16, starting transfers between devices, passed_along(): return lax.ppermute(x, axis, pairs)  72.6 us
    ppermute x16, waiting for transfers between devices, passed_along(): return lax.ppermute(x, axis, pairs)  44.3 us
    pallas_call x2, Pallas kernels, frame_grads(): pl.pallas_call(functools.partial(frames_kernel, last, len(pieces)), out_s...  32.4 us
    ppermute x6, starting transfers between devices, passed_around(): x = lax.ppermute(x, 'row', pairs)  20.7 us
    ppermute x6, waiting for transfers between devices, passed_around(): x = lax.ppermute(x, 'row', pairs)  7.4 us
  transfers between devices with their start and end apart: 22, of which 10 were waited for; matrix products, arithmetic and copies ran while one was open for 6% of the time, Pallas kernels for 0%

profile of v1, /device:TPU:23, one launch (start us, length us, event | category | flops | bytes accessed | tf_op | source)
XLA Modules:
  0.0 196.3 jit_solution(5264854417916232687)
XLA Ops:
  1.2 2.6 %collective-permute-start = (f32[4,384,128]{2,1,0:T(8,128)S(1)}, f32[4,384,128]{2,1,0:T(8,128)S(1)}, u32[]{:S(2)}, u32[]{:S(2)}) collective-permute-start(f32[4,384,128]{2,1,0:T(8,128)S(1)} %slice.156), channel_id=1, source_target_pairs={{1,0},{2,1},{3,2},{4,3},{5,4},{6,5},{7,6},{8,7},{9,8},{10,9},{11,1... | collective-permute-start | bytes 2359304 | tf_op jit(solution)/shard_map/ppermute | solution.py:264
  4.8 3.1 %collective-permute-start.3 = (f32[4,32,256]{2,1,0:T(8,128)S(1)}, f32[4,32,256]{2,1,0:T(8,128)S(1)}, u32[]{:S(2)}, u32[]{:S(2)}) collective-permute-start(f32[4,32,256]{2,1,0:T(8,128)S(1)} %slice.159), channel_id=1, source_target_pairs={{0,16},{16,32},{32,48},{48,0},{64,80},{80,96},{96,112},{112,64},{1... | collective-permute-start | bytes 393224 | tf_op jit(solution)/shard_map/ppermute | solution.py:257
  8.8 4.8 %collective-permute-start.1 = (f32[4,128,128]{2,1,0:T(8,128)S(1)}, f32[4,128,128]{2,1,0:T(8,128)S(1)}, u32[]{:S(2)}, u32[]{:S(2)}) collective-permute-start(f32[4,128,128]{2,1,0:T(8,128)S(1)} %slice.157), channel_id=1, source_target_pairs={{16,0},{32,16},{48,32},{64,48},{80,64},{96,80},{112,96},{128,112},... | collective-permute-start | bytes 786440 | tf_op jit(solution)/shard_map/ppermute | solution.py:264
  13.7 3.8 %collective-permute-done.3 = f32[4,32,256]{2,1,0:T(8,128)S(1)} collective-permute-done((f32[4,32,256]{2,1,0:T(8,128)S(1)}, f32[4,32,256]{2,1,0:T(8,128)S(1)}, u32[]{:S(2)}, u32[]{:S(2)}) %collective-permute-start.3) | collective-permute-done | bytes 131104 | tf_op jit(solution)/shard_map/ppermute | solution.py:257
  18.5 5.4 %collective-permute-start.2 = (f32[4,96,256]{2,1,0:T(8,128)S(1)}, f32[4,96,256]{2,1,0:T(8,128)S(1)}, u32[]{:S(2)}, u32[]{:S(2)}) collective-permute-start(f32[4,96,256]{2,1,0:T(8,128)S(1)} %slice.158), channel_id=1, source_target_pairs={{16,0},{32,16},{48,32},{64,48},{80,64},{96,80},{112,96},{128,112},... | collective-permute-start | bytes 1179656 | tf_op jit(solution)/shard_map/ppermute | solution.py:264
  23.8 2.1 %collective-permute-done.4 = f32[4,32,256]{2,1,0:T(8,128)S(1)} collective-permute-done((f32[4,32,256]{2,1,0:T(8,128)S(1)}, f32[4,32,256]{2,1,0:T(8,128)S(1)}, u32[]{:S(2)}, u32[]{:S(2)}) %collective-permute-start.4) | collective-permute-done | bytes 131104 | tf_op jit(solution)/shard_map/ppermute | solution.py:257
  25.9 2.7 %collective-permute-start.5 = (f32[4,32,256]{2,1,0:T(8,128)S(1)}, f32[4,32,256]{2,1,0:T(8,128)S(1)}, u32[]{:S(2)}, u32[]{:S(2)}) collective-permute-start(f32[4,32,256]{2,1,0:T(8,128)S(1)} %collective-permute-done.4), channel_id=1, source_target_pairs={{0,16},{16,32},{48,0},{64,80},{80,96},{96,48},{112,64},{128,144},{... | collective-permute-start | bytes 393224 | tf_op jit(solution)/shard_map/ppermute | solution.py:257
  28.6 15.3 %collective-permute-start.6 = (f32[4,128,128]{2,1,0:T(8,128)S(1)}, f32[4,128,128]{2,1,0:T(8,128)S(1)}, u32[]{:S(2)}, u32[]{:S(2)}) collective-permute-start(f32[4,128,128]{2,1,0:T(8,128)S(1)} %collective-permute-done.1.refs_2_), channel_id=1, source_target_pairs={{1,0},{2,1},{3,2},{4,3},{5,4},{6,5},{7,6},{8,7},{9,8},{10,9},{11,1... | collective-permute-start | bytes 786440 | tf_op jit(solution)/shard_map/ppermute | solution.py:264
  47.5 18.0 %frames.1 = (f32[4,4,4,128,128]{4,3,2,1,0:T(8,128)}, f32[4,3,4,128,128]{4,3,2,1,0:T(8,128)}) custom-call(s32[8,2]{1,0:T(8,128)} %copy.15.pos_ref, s32[1]{0:T(128)} %bitcast.cnt_ref, f32[4,384,384]{2,1,0:T(8,128)} %bitcast.75, f32[4,384,128]{2,1,0:T(8,128)} %copy-done.11, f32[4,128,128]{2,1,0:T(8,128)} %copy-done.13, f32[4,96,256]{2,1,0:T(8,128)} %copy-done.12, ...), custom_call_target="tpu_custom_call" | custom-call | flops 2000000000 | bytes 9000000 | tf_op jit(solution)/shard_map/frames/pallas_call | solution.py:226
  67.5 2.0 %collective-permute-start.9 = (f32[2,4,128,128]{3,2,1,0:T(8,128)}, f32[2,4,128,128]{3,2,1,0:T(8,128)}, u32[]{:S(2)}, u32[]{:S(2)}) collective-permute-start(f32[2,4,128,128]{3,2,1,0:T(8,128)} %pad_maximum_fusion), channel_id=1, source_target_pairs={{0,1},{1,2},{2,3},{3,4},{4,5},{5,6},{6,7},{7,8},{8,9},{9,10},{10,1... | collective-permute-start | bytes 1572872 | tf_op jit(solution)/shard_map/ppermute | solution.py:264
  69.5 1.9 slice_bitcast_fusion
  71.4 1.9 collective-permute-start.8
  74.7 6.7 %collective-permute-start.12 = (f32[2,4,128,128]{3,2,1,0:T(8,128)S(1)}, f32[2,4,128,128]{3,2,1,0:T(8,128)S(1)}, u32[]{:S(2)}, u32[]{:S(2)}) collective-permute-start(f32[2,4,128,128]{3,2,1,0:T(8,128)S(1)} %get-tuple-element.41), channel_id=1, source_target_pairs={{16,0},{32,16},{48,32},{64,48},{80,64},{96,80},{112,96},{128,112},... | collective-permute-start | bytes 1572872 | tf_op jit(solution)/shard_map/ppermute | solution.py:264
  81.3 1.9 collective-permute-start.7
  84.5 7.3 %collective-permute-start.13 = (f32[4,128,128]{2,1,0:T(8,128)S(1)}, f32[4,128,128]{2,1,0:T(8,128)S(1)}, u32[]{:S(2)}, u32[]{:S(2)}) collective-permute-start(f32[4,128,128]{2,1,0:T(8,128)S(1)} %get-tuple-element.39), channel_id=1, source_target_pairs={{16,0},{32,16},{48,32},{64,48},{80,64},{96,80},{112,96},{128,112},... | collective-permute-start | bytes 786440 | tf_op jit(solution)/shard_map/ppermute | solution.py:264
  91.8 1.9 collective-permute-start.10
  93.7 3.1 %collective-permute-done.8 = f32[2,4,128,128]{3,2,1,0:T(8,128)} collective-permute-done((f32[2,4,128,128]{3,2,1,0:T(8,128)}, f32[2,4,128,128]{3,2,1,0:T(8,128)}, u32[]{:S(2)}, u32[]{:S(2)}) %collective-permute-start.8) | collective-permute-done | bytes 524320 | tf_op jit(solution)/shard_map/ppermute | solution.py:264
  98.0 12.1 %collective-permute-start.11 = (f32[2,4,128,128]{3,2,1,0:T(8,128)S(1)}, f32[2,4,128,128]{3,2,1,0:T(8,128)S(1)}, u32[]{:S(2)}, u32[]{:S(2)}) collective-permute-start(f32[2,4,128,128]{3,2,1,0:T(8,128)S(1)} %fusion.3.refs_2_), channel_id=1, source_target_pairs={{1,0},{2,1},{3,2},{4,3},{5,4},{6,5},{7,6},{8,7},{9,8},{10,9},{11,1... | collective-permute-start | bytes 1572872 | tf_op jit(solution)/shard_map/ppermute | solution.py:264
  110.1 14.1 %collective-permute-done.10 = f32[4,128,128]{2,1,0:T(8,128)S(1)} collective-permute-done((f32[4,128,128]{2,1,0:T(8,128)S(1)}, f32[4,128,128]{2,1,0:T(8,128)S(1)}, u32[]{:S(2)}, u32[]{:S(2)}) %collective-permute-start.10) | collective-permute-done | bytes 262176 | tf_op jit(solution)/shard_map/ppermute | solution.py:264
  125.4 2.1 %collective-permute-start.14 = (f32[2,4,128,128]{3,2,1,0:T(8,128)S(1)}, f32[2,4,128,128]{3,2,1,0:T(8,128)S(1)}, u32[]{:S(2)}, u32[]{:S(2)}) collective-permute-start(f32[2,4,128,128]{3,2,1,0:T(8,128)S(1)} %pad_maximum_fusion.1), channel_id=1, source_target_pairs={{1,0},{2,1},{3,2},{4,3},{5,4},{6,5},{7,6},{8,7},{9,8},{10,9},{11,1... | collective-permute-start | bytes 1572872 | tf_op jit(solution)/shard_map/ppermute | solution.py:264
  127.7 8.3 %collective-permute-done.14.refs_7_ = f32[2,4,128,128]{3,2,1,0:T(8,128)S(1)} collective-permute-done((f32[2,4,128,128]{3,2,1,0:T(8,128)S(1)}, f32[2,4,128,128]{3,2,1,0:T(8,128)S(1)}, u32[]{:S(2)}, u32[]{:S(2)}) %collective-permute-start.14) | collective-permute-done | bytes 524320 | tf_op jit(solution)/shard_map/ppermute | solution.py:264
  136.1 14.4 %last_frames.1 = (f32[4,384,384]{2,1,0:T(8,128)}, f32[4,4,128,128]{3,2,1,0:T(8,128)S(1)}, f32[3,4,128,128]{3,2,1,0:T(8,128)S(1)}) custom-call(s32[8,2]{1,0:T(8,128)S(1)} %copy-done.2, s32[1]{0:T(128)} %bitcast.cnt_ref, f32[4,4,128,128]{3,2,1,0:T(8,128)S(1)} %bitcast.69, f32[2,4,128,128]{3,2,1,0:T(8,128)S(1)} %get-tuple-element.48.refs_1_, ...), custom_call_target="tpu_custom_call" | custom-call | flops 2000000000 | bytes 9000000 | tf_op jit(solution)/shard_map/last_frames/pallas_call | solution.py:226
  150.6 2.9 %collective-permute-start.18 = (f32[2,4,32,128]{3,2,1,0:T(8,128)S(1)}, f32[2,4,32,128]{3,2,1,0:T(8,128)S(1)}, u32[]{:S(2)}, u32[]{:S(2)}) collective-permute-start(f32[2,4,32,128]{3,2,1,0:T(8,128)S(1)} %slice.151), channel_id=1, source_target_pairs={{0,48},{16,0},{32,16},{48,32},{64,112},{80,64},{96,80},{112,96},{1... | collective-permute-start | bytes 393224 | tf_op jit(solution)/shard_map/ppermute | solution.py:257
  153.5 2.6 %collective-permute-start.15 = (f32[4,128,128]{2,1,0:T(8,128)S(1)}, f32[4,128,128]{2,1,0:T(8,128)S(1)}, u32[]{:S(2)}, u32[]{:S(2)}) collective-permute-start(f32[4,128,128]{2,1,0:T(8,128)S(1)} %slice_bitcast_fusion.8), channel_id=1, source_target_pairs={{0,1},{1,2},{2,3},{3,4},{4,5},{5,6},{6,7},{7,8},{8,9},{9,10},{10,1... | collective-permute-start | bytes 786440 | tf_op jit(solution)/shard_map/ppermute | solution.py:264
  156.1 1.9 collective-permute-start.17
  159.3 4.5 %collective-permute-start.19 = (f32[2,4,32,128]{3,2,1,0:T(8,128)S(1)}, f32[2,4,32,128]{3,2,1,0:T(8,128)S(1)}, u32[]{:S(2)}, u32[]{:S(2)}) collective-permute-start(f32[2,4,32,128]{3,2,1,0:T(8,128)S(1)} %collective-permute-done.18), channel_id=1, source_target_pairs={{0,48},{16,0},{32,16},{48,32},{64,112},{80,64},{96,80},{112,96},{1... | collective-permute-start | bytes 393224 | tf_op jit(solution)/shard_map/ppermute | solution.py:257
  163.8 2.3 %collective-permute-start.21 = (f32[3,4,128,128]{3,2,1,0:T(8,128)S(1)}, f32[3,4,128,128]{3,2,1,0:T(8,128)S(1)}, u32[]{:S(2)}, u32[]{:S(2)}) collective-permute-start(f32[3,4,128,128]{3,2,1,0:T(8,128)S(1)} %slice.155), channel_id=1, source_target_pairs={{0,1},{1,2},{2,3},{3,4},{4,5},{5,6},{6,7},{7,8},{8,9},{9,10},{10,1... | collective-permute-start | bytes 2359304 | tf_op jit(solution)/shard_map/ppermute | solution.py:264
  166.4 7.5 %collective-permute-start.20 = (f32[2,4,32,128]{3,2,1,0:T(8,128)S(1)}, f32[2,4,32,128]{3,2,1,0:T(8,128)S(1)}, u32[]{:S(2)}, u32[]{:S(2)}) collective-permute-start(f32[2,4,32,128]{3,2,1,0:T(8,128)S(1)} %collective-permute-done.19), channel_id=1, source_target_pairs={{0,48},{16,64},{32,16},{48,32},{64,112},{80,128},{96,80},{112,96},... | collective-permute-start | bytes 393224 | tf_op jit(solution)/shard_map/ppermute | solution.py:257
  174.0 1.9 collective-permute-start.16
  175.9 2.6 %collective-permute-done.17 = f32[2,4,96,128]{3,2,1,0:T(8,128)S(1)} collective-permute-done((f32[2,4,96,128]{3,2,1,0:T(8,128)S(1)}, f32[2,4,96,128]{3,2,1,0:T(8,128)S(1)}, u32[]{:S(2)}, u32[]{:S(2)}) %collective-permute-start.17) | collective-permute-done | bytes 393248 | tf_op jit(solution)/shard_map/ppermute | solution.py:264
  178.6 15.8 %collective-permute-done.16 = f32[4,128,128]{2,1,0:T(8,128)S(1)} collective-permute-done((f32[4,128,128]{2,1,0:T(8,128)S(1)}, f32[4,128,128]{2,1,0:T(8,128)S(1)}, u32[]{:S(2)}, u32[]{:S(2)}) %collective-permute-start.16) | collective-permute-done | bytes 262176 | tf_op jit(solution)/shard_map/ppermute | solution.py:264
  194.9 1.4 copy-done.8
  (76 shorter events, 17.1 us)
Async XLA Ops:
  0.0 44.9 %copy-start = (s32[1,16]{1,0:T(1,128)S(1)}, s32[1,16]{1,0:T(1,128)}, u32[]{:S(2)}) copy-start(s32[1,16]{1,0:T(1,128)} %param.16) | copy-start | bytes 196
  0.0 43.9 %copy-start.9 = (f32[128,128]{1,0:T(8,128)S(1)}, f32[128,128]{1,0:T(8,128)}, u32[]{:S(2)}) copy-start(f32[128,128]{1,0:T(8,128)} %param.13) | copy-start | bytes 196612
  0.0 44.2 %copy-start.10 = (s32[8,2]{0,1:T(2,128)S(1)}, s32[8,2]{0,1:T(2,128)}, u32[]{:S(2)}) copy-start(s32[8,2]{0,1:T(2,128)} %param.15) | copy-start | bytes 196
  1.2 45.3 %collective-permute-start = (f32[4,384,128]{2,1,0:T(8,128)S(1)}, f32[4,384,128]{2,1,0:T(8,128)S(1)}, u32[]{:S(2)}, u32[]{:S(2)}) collective-permute-start(f32[4,384,128]{2,1,0:T(8,128)S(1)} %slice.156), channel_id=1, source_target_pairs={{1,0},{2,1},{3,2},{4,3},{5,4},{6,5},{7,6},{8,7},{9,8},{10,9},{11,1... | collective-permute-start | bytes 2359304 | tf_op jit(solution)/shard_map/ppermute | solution.py:264
  4.8 12.7 %collective-permute-start.3 = (f32[4,32,256]{2,1,0:T(8,128)S(1)}, f32[4,32,256]{2,1,0:T(8,128)S(1)}, u32[]{:S(2)}, u32[]{:S(2)}) collective-permute-start(f32[4,32,256]{2,1,0:T(8,128)S(1)} %slice.159), channel_id=1, source_target_pairs={{0,16},{16,32},{32,48},{48,0},{64,80},{80,96},{96,112},{112,64},{1... | collective-permute-start | bytes 393224 | tf_op jit(solution)/shard_map/ppermute | solution.py:257
  8.8 19.8 %collective-permute-start.1 = (f32[4,128,128]{2,1,0:T(8,128)S(1)}, f32[4,128,128]{2,1,0:T(8,128)S(1)}, u32[]{:S(2)}, u32[]{:S(2)}) collective-permute-start(f32[4,128,128]{2,1,0:T(8,128)S(1)} %slice.157), channel_id=1, source_target_pairs={{16,0},{32,16},{48,32},{64,48},{80,64},{96,80},{112,96},{128,112},... | collective-permute-start | bytes 786440 | tf_op jit(solution)/shard_map/ppermute | solution.py:264
  17.4 8.5 %collective-permute-start.4 = (f32[4,32,256]{2,1,0:T(8,128)S(1)}, f32[4,32,256]{2,1,0:T(8,128)S(1)}, u32[]{:S(2)}, u32[]{:S(2)}) collective-permute-start(f32[4,32,256]{2,1,0:T(8,128)S(1)} %collective-permute-done.3), channel_id=1, source_target_pairs={{0,16},{16,32},{32,48},{48,0},{64,80},{80,96},{96,112},{112,64},{1... | collective-permute-start | bytes 393224 | tf_op jit(solution)/shard_map/ppermute | solution.py:257
  18.5 27.7 %collective-permute-start.2 = (f32[4,96,256]{2,1,0:T(8,128)S(1)}, f32[4,96,256]{2,1,0:T(8,128)S(1)}, u32[]{:S(2)}, u32[]{:S(2)}) collective-permute-start(f32[4,96,256]{2,1,0:T(8,128)S(1)} %slice.158), channel_id=1, source_target_pairs={{16,0},{32,16},{48,32},{64,48},{80,64},{96,80},{112,96},{128,112},... | collective-permute-start | bytes 1179656 | tf_op jit(solution)/shard_map/ppermute | solution.py:264
  25.9 20.2 %collective-permute-start.5 = (f32[4,32,256]{2,1,0:T(8,128)S(1)}, f32[4,32,256]{2,1,0:T(8,128)S(1)}, u32[]{:S(2)}, u32[]{:S(2)}) collective-permute-start(f32[4,32,256]{2,1,0:T(8,128)S(1)} %collective-permute-done.4), channel_id=1, source_target_pairs={{0,16},{16,32},{48,0},{64,80},{80,96},{96,48},{112,64},{128,144},{... | collective-permute-start | bytes 393224 | tf_op jit(solution)/shard_map/ppermute | solution.py:257
  28.6 17.9 %copy-start.13 = (f32[4,128,128]{2,1,0:T(8,128)}, f32[4,128,128]{2,1,0:T(8,128)S(1)}, u32[]{:S(2)}) copy-start(f32[4,128,128]{2,1,0:T(8,128)S(1)} %collective-permute-done.1.refs_2_) | copy-start | bytes 786436
  28.6 17.9 %collective-permute-start.6 = (f32[4,128,128]{2,1,0:T(8,128)S(1)}, f32[4,128,128]{2,1,0:T(8,128)S(1)}, u32[]{:S(2)}, u32[]{:S(2)}) collective-permute-start(f32[4,128,128]{2,1,0:T(8,128)S(1)} %collective-permute-done.1.refs_2_), channel_id=1, source_target_pairs={{1,0},{2,1},{3,2},{4,3},{5,4},{6,5},{7,6},{8,7},{9,8},{10,9},{11,1... | collective-permute-start | bytes 786440 | tf_op jit(solution)/shard_map/ppermute | solution.py:264
  66.6 30.2 %copy-start.6 = (f32[4,3,4,128,128]{4,3,2,1,0:T(8,128)S(1)}, f32[4,3,4,128,128]{4,3,2,1,0:T(8,128)}, u32[]{:S(2)}) copy-start(f32[4,3,4,128,128]{4,3,2,1,0:T(8,128)} %get-tuple-element.34) | copy-start | bytes 9437188
  67.5 15.8 %collective-permute-start.9 = (f32[2,4,128,128]{3,2,1,0:T(8,128)}, f32[2,4,128,128]{3,2,1,0:T(8,128)}, u32[]{:S(2)}, u32[]{:S(2)}) collective-permute-start(f32[2,4,128,128]{3,2,1,0:T(8,128)} %pad_maximum_fusion), channel_id=1, source_target_pairs={{0,1},{1,2},{2,3},{3,4},{4,5},{5,6},{6,7},{7,8},{8,9},{9,10},{10,1... | collective-permute-start | bytes 1572872 | tf_op jit(solution)/shard_map/ppermute | solution.py:264
  71.4 25.4 %collective-permute-start.8 = (f32[2,4,128,128]{3,2,1,0:T(8,128)}, f32[2,4,128,128]{3,2,1,0:T(8,128)}, u32[]{:S(2)}, u32[]{:S(2)}) collective-permute-start(f32[2,4,128,128]{3,2,1,0:T(8,128)} %slice_bitcast_fusion), channel_id=1, source_target_pairs={{0,1},{1,2},{2,3},{3,4},{4,5},{5,6},{6,7},{7,8},{8,9},{9,10},{10,1... | collective-permute-start | bytes 1572872 | tf_op jit(solution)/shard_map/ppermute | solution.py:264
  74.7 52.9 %collective-permute-start.12 = (f32[2,4,128,128]{3,2,1,0:T(8,128)S(1)}, f32[2,4,128,128]{3,2,1,0:T(8,128)S(1)}, u32[]{:S(2)}, u32[]{:S(2)}) collective-permute-start(f32[2,4,128,128]{3,2,1,0:T(8,128)S(1)} %get-tuple-element.41), channel_id=1, source_target_pairs={{16,0},{32,16},{48,32},{64,48},{80,64},{96,80},{112,96},{128,112},... | collective-permute-start | bytes 1572872 | tf_op jit(solution)/shard_map/ppermute | solution.py:264
  81.3 46.2 %collective-permute-start.7 = (f32[2,4,128,128]{3,2,1,0:T(8,128)S(1)}, f32[2,4,128,128]{3,2,1,0:T(8,128)S(1)}, u32[]{:S(2)}, u32[]{:S(2)}) collective-permute-start(f32[2,4,128,128]{3,2,1,0:T(8,128)S(1)} %get-tuple-element.42), channel_id=1, source_target_pairs={{0,16},{16,32},{32,48},{48,64},{64,80},{80,96},{96,112},{112,128},... | collective-permute-start | bytes 1572872 | tf_op jit(solution)/shard_map/ppermute | solution.py:264
  84.5 25.6 %collective-permute-start.13 = (f32[4,128,128]{2,1,0:T(8,128)S(1)}, f32[4,128,128]{2,1,0:T(8,128)S(1)}, u32[]{:S(2)}, u32[]{:S(2)}) collective-permute-start(f32[4,128,128]{2,1,0:T(8,128)S(1)} %get-tuple-element.39), channel_id=1, source_target_pairs={{16,0},{32,16},{48,32},{64,48},{80,64},{96,80},{112,96},{128,112},... | collective-permute-start | bytes 786440 | tf_op jit(solution)/shard_map/ppermute | solution.py:264
  91.8 32.4 %collective-permute-start.10 = (f32[4,128,128]{2,1,0:T(8,128)S(1)}, f32[4,128,128]{2,1,0:T(8,128)S(1)}, u32[]{:S(2)}, u32[]{:S(2)}) collective-permute-start(f32[4,128,128]{2,1,0:T(8,128)S(1)} %get-tuple-element.40), channel_id=1, source_target_pairs={{0,16},{16,32},{32,48},{48,64},{64,80},{80,96},{96,112},{112,128},... | collective-permute-start | bytes 786440 | tf_op jit(solution)/shard_map/ppermute | solution.py:264
  98.0 29.8 %collective-permute-start.11 = (f32[2,4,128,128]{3,2,1,0:T(8,128)S(1)}, f32[2,4,128,128]{3,2,1,0:T(8,128)S(1)}, u32[]{:S(2)}, u32[]{:S(2)}) collective-permute-start(f32[2,4,128,128]{3,2,1,0:T(8,128)S(1)} %fusion.3.refs_2_), channel_id=1, source_target_pairs={{1,0},{2,1},{3,2},{4,3},{5,4},{6,5},{7,6},{8,7},{9,8},{10,9},{11,1... | collective-permute-start | bytes 1572872 | tf_op jit(solution)/shard_map/ppermute | solution.py:264
  125.3 10.7 %copy-start.1 = (f32[2,128,128]{2,1,0:T(8,128)S(1)}, f32[2,128,128]{2,1,0:T(8,128)}, u32[]{:S(2)}) copy-start(f32[2,128,128]{2,1,0:T(8,128)} %pad_maximum_fusion.2.refs_8_.refs_10_) | copy-start | bytes 393220
  125.3 10.7 %copy-start.2 = (s32[8,2]{1,0:T(8,128)S(1)}, s32[8,2]{1,0:T(8,128)}, u32[]{:S(2)}) copy-start(s32[8,2]{1,0:T(8,128)} %copy.15.pos_ref) | copy-start | bytes 196
  125.3 10.7 %copy-start.3 = (f32[8,128,128]{2,1,0:T(8,128)S(1)}, f32[8,128,128]{2,1,0:T(8,128)}, u32[]{:S(2)}) copy-start(f32[8,128,128]{2,1,0:T(8,128)} %refs_8_.1) | copy-start | bytes 1572868
  125.4 10.7 %copy-start.4 = (f32[2,128,128]{2,1,0:T(8,128)S(1)}, f32[2,128,128]{2,1,0:T(8,128)}, u32[]{:S(2)}) copy-start(f32[2,128,128]{2,1,0:T(8,128)} %refs_9_.2) | copy-start | bytes 393220
  125.4 10.6 %collective-permute-start.14 = (f32[2,4,128,128]{3,2,1,0:T(8,128)S(1)}, f32[2,4,128,128]{3,2,1,0:T(8,128)S(1)}, u32[]{:S(2)}, u32[]{:S(2)}) collective-permute-start(f32[2,4,128,128]{3,2,1,0:T(8,128)S(1)} %pad_maximum_fusion.1), channel_id=1, source_target_pairs={{1,0},{2,1},{3,2},{4,3},{5,4},{6,5},{7,6},{8,7},{9,8},{10,9},{11,1... | collective-permute-start | bytes 1572872 | tf_op jit(solution)/shard_map/ppermute | solution.py:264
  150.5 43.8 %copy-start.7 = (f32[4,384,384]{2,1,0:T(8,128)S(1)}, f32[4,384,384]{2,1,0:T(8,128)}, u32[]{:S(2)}) copy-start(f32[4,384,384]{2,1,0:T(8,128)} %get-tuple-element.36) | copy-start | bytes 7077892
  150.6 8.8 %collective-permute-start.18 = (f32[2,4,32,128]{3,2,1,0:T(8,128)S(1)}, f32[2,4,32,128]{3,2,1,0:T(8,128)S(1)}, u32[]{:S(2)}, u32[]{:S(2)}) collective-permute-start(f32[2,4,32,128]{3,2,1,0:T(8,128)S(1)} %slice.151), channel_id=1, source_target_pairs={{0,48},{16,0},{32,16},{48,32},{64,112},{80,64},{96,80},{112,96},{1... | collective-permute-start | bytes 393224 | tf_op jit(solution)/shard_map/ppermute | solution.py:257
  153.5 20.4 %collective-permute-start.15 = (f32[4,128,128]{2,1,0:T(8,128)S(1)}, f32[4,128,128]{2,1,0:T(8,128)S(1)}, u32[]{:S(2)}, u32[]{:S(2)}) collective-permute-start(f32[4,128,128]{2,1,0:T(8,128)S(1)} %slice_bitcast_fusion.8), channel_id=1, source_target_pairs={{0,1},{1,2},{2,3},{3,4},{4,5},{5,6},{6,7},{7,8},{8,9},{9,10},{10,1... | collective-permute-start | bytes 786440 | tf_op jit(solution)/shard_map/ppermute | solution.py:264
  156.1 22.3 %collective-permute-start.17 = (f32[2,4,96,128]{3,2,1,0:T(8,128)S(1)}, f32[2,4,96,128]{3,2,1,0:T(8,128)S(1)}, u32[]{:S(2)}, u32[]{:S(2)}) collective-permute-start(f32[2,4,96,128]{3,2,1,0:T(8,128)S(1)} %slice.150), channel_id=1, source_target_pairs={{0,16},{16,32},{32,48},{48,64},{64,80},{80,96},{96,112},{112,128},... | collective-permute-start | bytes 1179656 | tf_op jit(solution)/shard_map/ppermute | solution.py:264
  159.3 7.0 %collective-permute-start.19 = (f32[2,4,32,128]{3,2,1,0:T(8,128)S(1)}, f32[2,4,32,128]{3,2,1,0:T(8,128)S(1)}, u32[]{:S(2)}, u32[]{:S(2)}) collective-permute-start(f32[2,4,32,128]{3,2,1,0:T(8,128)S(1)} %collective-permute-done.18), channel_id=1, source_target_pairs={{0,48},{16,0},{32,16},{48,32},{64,112},{80,64},{96,80},{112,96},{1... | collective-permute-start | bytes 393224 | tf_op jit(solution)/shard_map/ppermute | solution.py:257
  163.8 30.7 %collective-permute-start.21 = (f32[3,4,128,128]{3,2,1,0:T(8,128)S(1)}, f32[3,4,128,128]{3,2,1,0:T(8,128)S(1)}, u32[]{:S(2)}, u32[]{:S(2)}) collective-permute-start(f32[3,4,128,128]{3,2,1,0:T(8,128)S(1)} %slice.155), channel_id=1, source_target_pairs={{0,1},{1,2},{2,3},{3,4},{4,5},{5,6},{6,7},{7,8},{8,9},{9,10},{10,1... | collective-permute-start | bytes 2359304 | tf_op jit(solution)/shard_map/ppermute | solution.py:264
  166.4 12.1 %collective-permute-start.20 = (f32[2,4,32,128]{3,2,1,0:T(8,128)S(1)}, f32[2,4,32,128]{3,2,1,0:T(8,128)S(1)}, u32[]{:S(2)}, u32[]{:S(2)}) collective-permute-start(f32[2,4,32,128]{3,2,1,0:T(8,128)S(1)} %collective-permute-done.19), channel_id=1, source_target_pairs={{0,48},{16,64},{32,16},{48,32},{64,112},{80,128},{96,80},{112,96},... | collective-permute-start | bytes 393224 | tf_op jit(solution)/shard_map/ppermute | solution.py:257
  174.0 20.4 %collective-permute-start.16 = (f32[4,128,128]{2,1,0:T(8,128)S(1)}, f32[4,128,128]{2,1,0:T(8,128)S(1)}, u32[]{:S(2)}, u32[]{:S(2)}) collective-permute-start(f32[4,128,128]{2,1,0:T(8,128)S(1)} %bitcast_add_fusion), channel_id=1, source_target_pairs={{0,16},{16,32},{32,48},{48,64},{64,80},{80,96},{96,112},{112,128},... | collective-permute-start | bytes 786440 | tf_op jit(solution)/shard_map/ppermute | solution.py:264
  (6 other events, 15.3 us)

commit v2 on v1

--- a/solution.py
+++ b/solution.py
@@ -236,7 +236,7 @@
             pltpu.SemaphoreType.DMA((24,)),
             pltpu.SemaphoreType.DMA,
         ],
-        compiler_params=pltpu.CompilerParams(vmem_limit_bytes=(32 if last else 60) * 1024 * 1024),
+        compiler_params=pltpu.CompilerParams(vmem_limit_bytes=(32 if last else 50) * 1024 * 1024),
         cost_estimate=pl.CostEstimate(flops=2 * 10**9, bytes_accessed=9 * 10**6, transcendentals=0),
         name="last_frames" if last else "frames",
     )(positions, count, *pieces, intensity, probe_field, kern, tab)

time: 200 us -> 197 us (0.985)
  other arithmetic: 5.72 us -> 2.86 us
    ppermute x16, starting transfers between devices: 72.6 us -> 78.6 us  [passed_along(): return lax.ppermute(x, axis, pairs)]
    ppermute x6, starting transfers between devices: 20.7 us -> 15.9 us  [passed_around(): x = lax.ppermute(x, 'row', pairs)]
  transfers between devices with their start and end apart: 22 -> 22, of which waited for: 10 -> 8; matrix products, arithmetic and copies ran while one was open for 6% -> 5% of each run, Pallas kernels for 0% -> 0%
where the time goes in v2:
time: 197 us; the launch traced here: 193 us
  starting transfers between devices  94.5 us (48%)
  waiting for transfers between devices  51.8 us (26%)
  Pallas kernels  31.3 us (16%)
  local copies, waits for them, and re-layouts  11.9 us (6%)
  other arithmetic  2.86 us (1%)
    ppermute x16, starting transfers between devices, passed_along(): return lax.ppermute(x, axis, pairs)  78.6 us
    ppermute x16, waiting for transfers between devices, passed_along(): return lax.ppermute(x, axis, pairs)  43.7 us
    pallas_call x2, Pallas kernels, frame_grads(): pl.pallas_call(functools.partial(frames_kernel, last, len(pieces)), out_s...  31.3 us
    ppermute x6, starting transfers between devices, passed_around(): x = lax.ppermute(x, 'row', pairs)  15.9 us
    ppermute x6, waiting for transfers between devices, passed_around(): x = lax.ppermute(x, 'row', pairs)  8.09 us
  transfers between devices with their start and end apart: 22, of which 8 were waited for; matrix products, arithmetic and copies ran while one was open for 5% of the time, Pallas kernels for 0%

profile of v2, /device:TPU:23, one launch (start us, length us, event | category | flops | bytes accessed | tf_op | source)
XLA Modules:
  0.0 192.9 jit_solution(1548255340975512384)
XLA Ops:
  0.0 2.2 %slice.156 = f32[4,384,128]{2,1,0:T(8,128)} slice(f32[4,384,384]{2,1,0:T(8,128)} %bitcast.71), slice={[0:4], [0:384], [0:128]} | slice | bytes 1572864 | tf_op jit(solution)/shard_map/slice | solution.py:278
  2.2 2.6 %collective-permute-start = (f32[4,384,128]{2,1,0:T(8,128)}, f32[4,384,128]{2,1,0:T(8,128)S(1)}, u32[]{:S(2)}, u32[]{:S(2)}) collective-permute-start(f32[4,384,128]{2,1,0:T(8,128)} %slice.156), channel_id=1, source_target_pairs={{1,0},{2,1},{3,2},{4,3},{5,4},{6,5},{7,6},{8,7},{9,8},{10,9},{11,1... | collective-permute-start | bytes 2359304 | tf_op jit(solution)/shard_map/ppermute | solution.py:264
  5.7 3.1 %collective-permute-start.3 = (f32[4,32,256]{2,1,0:T(8,128)S(1)}, f32[4,32,256]{2,1,0:T(8,128)S(1)}, u32[]{:S(2)}, u32[]{:S(2)}) collective-permute-start(f32[4,32,256]{2,1,0:T(8,128)S(1)} %slice.159), channel_id=1, source_target_pairs={{0,16},{16,32},{32,48},{48,0},{64,80},{80,96},{96,112},{112,64},{1... | collective-permute-start | bytes 393224 | tf_op jit(solution)/shard_map/ppermute | solution.py:257
  9.8 4.8 %collective-permute-start.1 = (f32[4,128,128]{2,1,0:T(8,128)S(1)}, f32[4,128,128]{2,1,0:T(8,128)S(1)}, u32[]{:S(2)}, u32[]{:S(2)}) collective-permute-start(f32[4,128,128]{2,1,0:T(8,128)S(1)} %slice.157), channel_id=1, source_target_pairs={{16,0},{32,16},{48,32},{64,48},{80,64},{96,80},{112,96},{128,112},... | collective-permute-start | bytes 786440 | tf_op jit(solution)/shard_map/ppermute | solution.py:264
  14.6 3.7 %collective-permute-done.3 = f32[4,32,256]{2,1,0:T(8,128)S(1)} collective-permute-done((f32[4,32,256]{2,1,0:T(8,128)S(1)}, f32[4,32,256]{2,1,0:T(8,128)S(1)}, u32[]{:S(2)}, u32[]{:S(2)}) %collective-permute-start.3) | collective-permute-done | bytes 131104 | tf_op jit(solution)/shard_map/ppermute | solution.py:257
  19.4 5.3 %collective-permute-start.2 = (f32[4,96,256]{2,1,0:T(8,128)S(1)}, f32[4,96,256]{2,1,0:T(8,128)S(1)}, u32[]{:S(2)}, u32[]{:S(2)}) collective-permute-start(f32[4,96,256]{2,1,0:T(8,128)S(1)} %slice.158), channel_id=1, source_target_pairs={{16,0},{32,16},{48,32},{64,48},{80,64},{96,80},{112,96},{128,112},... | collective-permute-start | bytes 1179656 | tf_op jit(solution)/shard_map/ppermute | solution.py:264
  24.7 2.3 %collective-permute-done.4 = f32[4,32,256]{2,1,0:T(8,128)} collective-permute-done((f32[4,32,256]{2,1,0:T(8,128)S(1)}, f32[4,32,256]{2,1,0:T(8,128)}, u32[]{:S(2)}, u32[]{:S(2)}) %collective-permute-start.4) | collective-permute-done | bytes 131104 | tf_op jit(solution)/shard_map/ppermute | solution.py:257
  27.0 2.5 %collective-permute-start.5 = (f32[4,32,256]{2,1,0:T(8,128)}, f32[4,32,256]{2,1,0:T(8,128)S(1)}, u32[]{:S(2)}, u32[]{:S(2)}) collective-permute-start(f32[4,32,256]{2,1,0:T(8,128)} %collective-permute-done.4), channel_id=1, source_target_pairs={{0,16},{16,32},{48,0},{64,80},{80,96},{96,48},{112,64},{128,144},{... | collective-permute-start | bytes 393224 | tf_op jit(solution)/shard_map/ppermute | solution.py:257
  29.6 15.5 %collective-permute-start.6 = (f32[4,128,128]{2,1,0:T(8,128)S(1)}, f32[4,128,128]{2,1,0:T(8,128)S(1)}, u32[]{:S(2)}, u32[]{:S(2)}) collective-permute-start(f32[4,128,128]{2,1,0:T(8,128)S(1)} %collective-permute-done.1.refs_2_), channel_id=1, source_target_pairs={{1,0},{2,1},{3,2},{4,3},{5,4},{6,5},{7,6},{8,7},{9,8},{10,9},{11,1... | collective-permute-start | bytes 786440 | tf_op jit(solution)/shard_map/ppermute | solution.py:264
  47.6 16.9 %frames.1 = (f32[4,4,4,128,128]{4,3,2,1,0:T(8,128)}, f32[4,3,4,128,128]{4,3,2,1,0:T(8,128)}) custom-call(s32[8,2]{1,0:T(8,128)S(1)} %copy.15.pos_ref, s32[1]{0:T(128)} %bitcast.cnt_ref, f32[4,384,384]{2,1,0:T(8,128)} %bitcast.75, f32[4,384,128]{2,1,0:T(8,128)S(1)} %collective-permute-done.refs_1_, f32[4,128,128]{2,1,0:T(8,128)S(1)} %collective-permute-done.1.refs_2_, ...), custom_call_target="tpu_custom_call" | custom-call | flops 2000000000 | bytes 9000000 | tf_op jit(solution)/shard_map/frames/pallas_call | solution.py:226
  65.7 1.9 collective-permute-start.9
  68.7 1.9 collective-permute-start.8
  70.6 1.4 slice_bitcast_fusion.2
  72.1 6.9 %collective-permute-start.12 = (f32[2,4,128,128]{3,2,1,0:T(8,128)S(1)}, f32[2,4,128,128]{3,2,1,0:T(8,128)S(1)}, u32[]{:S(2)}, u32[]{:S(2)}) collective-permute-start(f32[2,4,128,128]{3,2,1,0:T(8,128)S(1)} %get-tuple-element.41), channel_id=1, source_target_pairs={{16,0},{32,16},{48,32},{64,48},{80,64},{96,80},{112,96},{128,112},... | collective-permute-start | bytes 1572872 | tf_op jit(solution)/shard_map/ppermute | solution.py:264
  79.0 1.9 collective-permute-start.7
  82.0 7.2 %collective-permute-start.13 = (f32[4,128,128]{2,1,0:T(8,128)S(1)}, f32[4,128,128]{2,1,0:T(8,128)S(1)}, u32[]{:S(2)}, u32[]{:S(2)}) collective-permute-start(f32[4,128,128]{2,1,0:T(8,128)S(1)} %get-tuple-element.39), channel_id=1, source_target_pairs={{16,0},{32,16},{48,32},{64,48},{80,64},{96,80},{112,96},{128,112},... | collective-permute-start | bytes 786440 | tf_op jit(solution)/shard_map/ppermute | solution.py:264
  89.3 7.5 %collective-permute-start.10 = (f32[4,128,128]{2,1,0:T(8,128)S(1)}, f32[4,128,128]{2,1,0:T(8,128)S(1)}, u32[]{:S(2)}, u32[]{:S(2)}) collective-permute-start(f32[4,128,128]{2,1,0:T(8,128)S(1)} %get-tuple-element.40), channel_id=1, source_target_pairs={{0,16},{16,32},{32,48},{48,64},{64,80},{80,96},{96,112},{112,128},... | collective-permute-start | bytes 786440 | tf_op jit(solution)/shard_map/ppermute | solution.py:264
  96.9 11.6 %collective-permute-start.11 = (f32[2,4,128,128]{3,2,1,0:T(8,128)S(1)}, f32[2,4,128,128]{3,2,1,0:T(8,128)S(1)}, u32[]{:S(2)}, u32[]{:S(2)}) collective-permute-start(f32[2,4,128,128]{3,2,1,0:T(8,128)S(1)} %fusion.3.refs_2_), channel_id=1, source_target_pairs={{1,0},{2,1},{3,2},{4,3},{5,4},{6,5},{7,6},{8,7},{9,8},{10,9},{11,1... | collective-permute-start | bytes 1572872 | tf_op jit(solution)/shard_map/ppermute | solution.py:264
  108.5 15.3 %collective-permute-done.10 = f32[4,128,128]{2,1,0:T(8,128)S(1)} collective-permute-done((f32[4,128,128]{2,1,0:T(8,128)S(1)}, f32[4,128,128]{2,1,0:T(8,128)S(1)}, u32[]{:S(2)}, u32[]{:S(2)}) %collective-permute-start.10) | collective-permute-done | bytes 262176 | tf_op jit(solution)/shard_map/ppermute | solution.py:264
  123.9 1.9 collective-permute-start.14
  126.1 8.3 %collective-permute-done.14.refs_7_ = f32[2,4,128,128]{3,2,1,0:T(8,128)S(1)} collective-permute-done((f32[2,4,128,128]{3,2,1,0:T(8,128)S(1)}, f32[2,4,128,128]{3,2,1,0:T(8,128)S(1)}, u32[]{:S(2)}, u32[]{:S(2)}) %collective-permute-start.14) | collective-permute-done | bytes 524320 | tf_op jit(solution)/shard_map/ppermute | solution.py:264
  134.4 14.4 %last_frames.1 = (f32[4,384,384]{2,1,0:T(8,128)}, f32[4,4,128,128]{3,2,1,0:T(8,128)S(1)}, f32[3,4,128,128]{3,2,1,0:T(8,128)S(1)}) custom-call(s32[8,2]{1,0:T(8,128)S(1)} %copy.15.pos_ref, s32[1]{0:T(128)} %bitcast.cnt_ref, f32[4,4,128,128]{3,2,1,0:T(8,128)S(1)} %bitcast.69, f32[2,4,128,128]{3,2,1,0:T(8,128)S(1)} %get-tuple-element.48.refs_1_, ...), custom_call_target="tpu_custom_call" | custom-call | flops 2000000000 | bytes 9000000 | tf_op jit(solution)/shard_map/last_frames/pallas_call | solution.py:226
  150.0 1.9 collective-permute-start.15
  152.0 3.4 %collective-permute-start.17 = (f32[2,4,96,128]{3,2,1,0:T(8,128)S(1)}, f32[2,4,96,128]{3,2,1,0:T(8,128)S(1)}, u32[]{:S(2)}, u32[]{:S(2)}) collective-permute-start(f32[2,4,96,128]{3,2,1,0:T(8,128)S(1)} %slice.150), channel_id=1, source_target_pairs={{0,16},{16,32},{32,48},{48,64},{64,80},{80,96},{96,112},{112,128},... | collective-permute-start | bytes 1179656 | tf_op jit(solution)/shard_map/ppermute | solution.py:264
  156.1 4.0 %collective-permute-start.19 = (f32[2,4,32,128]{3,2,1,0:T(8,128)S(1)}, f32[2,4,32,128]{3,2,1,0:T(8,128)S(1)}, u32[]{:S(2)}, u32[]{:S(2)}) collective-permute-start(f32[2,4,32,128]{3,2,1,0:T(8,128)S(1)} %collective-permute-done.18), channel_id=1, source_target_pairs={{0,48},{16,0},{32,16},{48,32},{64,112},{80,64},{96,80},{112,96},{1... | collective-permute-start | bytes 393224 | tf_op jit(solution)/shard_map/ppermute | solution.py:257
  160.1 1.9 collective-permute-start.21
  162.0 1.4 collective-permute-done.19
  163.5 5.1 %collective-permute-start.20 = (f32[2,4,32,128]{3,2,1,0:T(8,128)S(1)}, f32[2,4,32,128]{3,2,1,0:T(8,128)S(1)}, u32[]{:S(2)}, u32[]{:S(2)}) collective-permute-start(f32[2,4,32,128]{3,2,1,0:T(8,128)S(1)} %collective-permute-done.19), channel_id=1, source_target_pairs={{0,48},{16,64},{32,16},{48,32},{64,112},{80,128},{96,80},{112,96},... | collective-permute-start | bytes 393224 | tf_op jit(solution)/shard_map/ppermute | solution.py:257
  168.6 2.2 %collective-permute-start.16 = (f32[4,128,128]{2,1,0:T(8,128)S(1)}, f32[4,128,128]{2,1,0:T(8,128)S(1)}, u32[]{:S(2)}, u32[]{:S(2)}) collective-permute-start(f32[4,128,128]{2,1,0:T(8,128)S(1)} %bitcast_add_fusion), channel_id=1, source_target_pairs={{0,16},{16,32},{32,48},{48,64},{64,80},{80,96},{96,112},{112,128},... | collective-permute-start | bytes 786440 | tf_op jit(solution)/shard_map/ppermute | solution.py:264
  170.8 4.3 %collective-permute-done.17 = f32[2,4,96,128]{3,2,1,0:T(8,128)S(1)} collective-permute-done((f32[2,4,96,128]{3,2,1,0:T(8,128)S(1)}, f32[2,4,96,128]{3,2,1,0:T(8,128)S(1)}, u32[]{:S(2)}, u32[]{:S(2)}) %collective-permute-start.17) | collective-permute-done | bytes 393248 | tf_op jit(solution)/shard_map/ppermute | solution.py:264
  175.2 15.8 %collective-permute-done.16 = f32[4,128,128]{2,1,0:T(8,128)S(1)} collective-permute-done((f32[4,128,128]{2,1,0:T(8,128)S(1)}, f32[4,128,128]{2,1,0:T(8,128)S(1)}, u32[]{:S(2)}, u32[]{:S(2)}) %collective-permute-start.16) | collective-permute-done | bytes 262176 | tf_op jit(solution)/shard_map/ppermute | solution.py:264
  191.5 1.4 copy-done.6
  (62 shorter events, 11.7 us)
Async XLA Ops:
  0.0 46.1 %copy-start = (s32[1,16]{1,0:T(1,128)S(1)}, s32[1,16]{1,0:T(1,128)}, u32[]{:S(2)}) copy-start(s32[1,16]{1,0:T(1,128)} %param.16) | copy-start | bytes 196
  0.0 47.6 %copy-start.3 = (bf16[4,256,256]{2,1,0:T(8,128)(2,1)S(1)}, bf16[4,256,256]{2,1,0:T(8,128)(2,1)}, u32[]{:S(2)}) copy-start(bf16[4,256,256]{2,1,0:T(8,128)(2,1)} %constant.72.clone.refs_9_.refs_11_) | copy-start | bytes 1572868
  0.0 45.1 %copy-start.7 = (f32[128,128]{1,0:T(8,128)S(1)}, f32[128,128]{1,0:T(8,128)}, u32[]{:S(2)}) copy-start(f32[128,128]{1,0:T(8,128)} %param.13) | copy-start | bytes 196612
  0.0 46.0 %copy-start.8 = (s32[8,2]{0,1:T(2,128)S(1)}, s32[8,2]{0,1:T(2,128)}, u32[]{:S(2)}) copy-start(s32[8,2]{0,1:T(2,128)} %param.15) | copy-start | bytes 196
  0.0 47.5 %copy-start.1 = (f32[8,128,128]{2,1,0:T(8,128)S(1)}, f32[8,128,128]{2,1,0:T(8,128)}, u32[]{:S(2)}) copy-start(f32[8,128,128]{2,1,0:T(8,128)} %refs_8_.1) | copy-start | bytes 1572868
  0.0 47.5 %copy-start.2 = (f32[2,128,128]{2,1,0:T(8,128)S(1)}, f32[2,128,128]{2,1,0:T(8,128)}, u32[]{:S(2)}) copy-start(f32[2,128,128]{2,1,0:T(8,128)} %refs_9_.2) | copy-start | bytes 393220
  2.2 45.3 %collective-permute-start = (f32[4,384,128]{2,1,0:T(8,128)}, f32[4,384,128]{2,1,0:T(8,128)S(1)}, u32[]{:S(2)}, u32[]{:S(2)}) collective-permute-start(f32[4,384,128]{2,1,0:T(8,128)} %slice.156), channel_id=1, source_target_pairs={{1,0},{2,1},{3,2},{4,3},{5,4},{6,5},{7,6},{8,7},{9,8},{10,9},{11,1... | collective-permute-start | bytes 2359304 | tf_op jit(solution)/shard_map/ppermute | solution.py:264
  5.7 12.6 %collective-permute-start.3 = (f32[4,32,256]{2,1,0:T(8,128)S(1)}, f32[4,32,256]{2,1,0:T(8,128)S(1)}, u32[]{:S(2)}, u32[]{:S(2)}) collective-permute-start(f32[4,32,256]{2,1,0:T(8,128)S(1)} %slice.159), channel_id=1, source_target_pairs={{0,16},{16,32},{32,48},{48,0},{64,80},{80,96},{96,112},{112,64},{1... | collective-permute-start | bytes 393224 | tf_op jit(solution)/shard_map/ppermute | solution.py:257
  9.8 19.8 %collective-permute-start.1 = (f32[4,128,128]{2,1,0:T(8,128)S(1)}, f32[4,128,128]{2,1,0:T(8,128)S(1)}, u32[]{:S(2)}, u32[]{:S(2)}) collective-permute-start(f32[4,128,128]{2,1,0:T(8,128)S(1)} %slice.157), channel_id=1, source_target_pairs={{16,0},{32,16},{48,32},{64,48},{80,64},{96,80},{112,96},{128,112},... | collective-permute-start | bytes 786440 | tf_op jit(solution)/shard_map/ppermute | solution.py:264
  18.3 8.7 %collective-permute-start.4 = (f32[4,32,256]{2,1,0:T(8,128)S(1)}, f32[4,32,256]{2,1,0:T(8,128)}, u32[]{:S(2)}, u32[]{:S(2)}) collective-permute-start(f32[4,32,256]{2,1,0:T(8,128)S(1)} %collective-permute-done.3), channel_id=1, source_target_pairs={{0,16},{16,32},{32,48},{48,0},{64,80},{80,96},{96,112},{112,64},{1... | collective-permute-start | bytes 393224 | tf_op jit(solution)/shard_map/ppermute | solution.py:257
  19.4 28.1 %collective-permute-start.2 = (f32[4,96,256]{2,1,0:T(8,128)S(1)}, f32[4,96,256]{2,1,0:T(8,128)S(1)}, u32[]{:S(2)}, u32[]{:S(2)}) collective-permute-start(f32[4,96,256]{2,1,0:T(8,128)S(1)} %slice.158), channel_id=1, source_target_pairs={{16,0},{32,16},{48,32},{64,48},{80,64},{96,80},{112,96},{128,112},... | collective-permute-start | bytes 1179656 | tf_op jit(solution)/shard_map/ppermute | solution.py:264
  27.0 20.5 %collective-permute-start.5 = (f32[4,32,256]{2,1,0:T(8,128)}, f32[4,32,256]{2,1,0:T(8,128)S(1)}, u32[]{:S(2)}, u32[]{:S(2)}) collective-permute-start(f32[4,32,256]{2,1,0:T(8,128)} %collective-permute-done.4), channel_id=1, source_target_pairs={{0,16},{16,32},{48,0},{64,80},{80,96},{96,48},{112,64},{128,144},{... | collective-permute-start | bytes 393224 | tf_op jit(solution)/shard_map/ppermute | solution.py:257
  29.6 18.0 %collective-permute-start.6 = (f32[4,128,128]{2,1,0:T(8,128)S(1)}, f32[4,128,128]{2,1,0:T(8,128)S(1)}, u32[]{:S(2)}, u32[]{:S(2)}) collective-permute-start(f32[4,128,128]{2,1,0:T(8,128)S(1)} %collective-permute-done.1.refs_2_), channel_id=1, source_target_pairs={{1,0},{2,1},{3,2},{4,3},{5,4},{6,5},{7,6},{8,7},{9,8},{10,9},{11,1... | collective-permute-start | bytes 786440 | tf_op jit(solution)/shard_map/ppermute | solution.py:264
  65.7 15.3 %collective-permute-start.9 = (f32[2,4,128,128]{3,2,1,0:T(8,128)S(1)}, f32[2,4,128,128]{3,2,1,0:T(8,128)S(1)}, u32[]{:S(2)}, u32[]{:S(2)}) collective-permute-start(f32[2,4,128,128]{3,2,1,0:T(8,128)S(1)} %pad_maximum_fusion), channel_id=1, source_target_pairs={{0,1},{1,2},{2,3},{3,4},{4,5},{5,6},{6,7},{7,8},{8,9},{9,10},{10,1... | collective-permute-start | bytes 1572872 | tf_op jit(solution)/shard_map/ppermute | solution.py:264
  68.7 28.1 %collective-permute-start.8 = (f32[2,4,128,128]{3,2,1,0:T(8,128)S(1)}, f32[2,4,128,128]{3,2,1,0:T(8,128)S(1)}, u32[]{:S(2)}, u32[]{:S(2)}) collective-permute-start(f32[2,4,128,128]{3,2,1,0:T(8,128)S(1)} %slice_bitcast_fusion), channel_id=1, source_target_pairs={{0,1},{1,2},{2,3},{3,4},{4,5},{5,6},{6,7},{7,8},{8,9},{9,10},{10,1... | collective-permute-start | bytes 1572872 | tf_op jit(solution)/shard_map/ppermute | solution.py:264
  70.6 26.2 %copy-start.4 = (f32[4,3,4,128,128]{4,3,2,1,0:T(8,128)S(1)}, f32[4,3,4,128,128]{4,3,2,1,0:T(8,128)}, u32[]{:S(2)}) copy-start(f32[4,3,4,128,128]{4,3,2,1,0:T(8,128)} %get-tuple-element.34) | copy-start | bytes 9437188
  72.1 53.9 %collective-permute-start.12 = (f32[2,4,128,128]{3,2,1,0:T(8,128)S(1)}, f32[2,4,128,128]{3,2,1,0:T(8,128)S(1)}, u32[]{:S(2)}, u32[]{:S(2)}) collective-permute-start(f32[2,4,128,128]{3,2,1,0:T(8,128)S(1)} %get-tuple-element.41), channel_id=1, source_target_pairs={{16,0},{32,16},{48,32},{64,48},{80,64},{96,80},{112,96},{128,112},... | collective-permute-start | bytes 1572872 | tf_op jit(solution)/shard_map/ppermute | solution.py:264
  79.0 47.0 %collective-permute-start.7 = (f32[2,4,128,128]{3,2,1,0:T(8,128)S(1)}, f32[2,4,128,128]{3,2,1,0:T(8,128)S(1)}, u32[]{:S(2)}, u32[]{:S(2)}) collective-permute-start(f32[2,4,128,128]{3,2,1,0:T(8,128)S(1)} %get-tuple-element.42), channel_id=1, source_target_pairs={{0,16},{16,32},{32,48},{48,64},{64,80},{80,96},{96,112},{112,128},... | collective-permute-start | bytes 1572872 | tf_op jit(solution)/shard_map/ppermute | solution.py:264
  82.0 26.5 %collective-permute-start.13 = (f32[4,128,128]{2,1,0:T(8,128)S(1)}, f32[4,128,128]{2,1,0:T(8,128)S(1)}, u32[]{:S(2)}, u32[]{:S(2)}) collective-permute-start(f32[4,128,128]{2,1,0:T(8,128)S(1)} %get-tuple-element.39), channel_id=1, source_target_pairs={{16,0},{32,16},{48,32},{64,48},{80,64},{96,80},{112,96},{128,112},... | collective-permute-start | bytes 786440 | tf_op jit(solution)/shard_map/ppermute | solution.py:264
  89.3 34.5 %collective-permute-start.10 = (f32[4,128,128]{2,1,0:T(8,128)S(1)}, f32[4,128,128]{2,1,0:T(8,128)S(1)}, u32[]{:S(2)}, u32[]{:S(2)}) collective-permute-start(f32[4,128,128]{2,1,0:T(8,128)S(1)} %get-tuple-element.40), channel_id=1, source_target_pairs={{0,16},{16,32},{32,48},{48,64},{64,80},{80,96},{96,112},{112,128},... | collective-permute-start | bytes 786440 | tf_op jit(solution)/shard_map/ppermute | solution.py:264
  96.9 29.2 %collective-permute-start.11 = (f32[2,4,128,128]{3,2,1,0:T(8,128)S(1)}, f32[2,4,128,128]{3,2,1,0:T(8,128)S(1)}, u32[]{:S(2)}, u32[]{:S(2)}) collective-permute-start(f32[2,4,128,128]{3,2,1,0:T(8,128)S(1)} %fusion.3.refs_2_), channel_id=1, source_target_pairs={{1,0},{2,1},{3,2},{4,3},{5,4},{6,5},{7,6},{8,7},{9,8},{10,9},{11,1... | collective-permute-start | bytes 1572872 | tf_op jit(solution)/shard_map/ppermute | solution.py:264
  123.9 10.5 %collective-permute-start.14 = (f32[2,4,128,128]{3,2,1,0:T(8,128)S(1)}, f32[2,4,128,128]{3,2,1,0:T(8,128)S(1)}, u32[]{:S(2)}, u32[]{:S(2)}) collective-permute-start(f32[2,4,128,128]{3,2,1,0:T(8,128)S(1)} %pad_maximum_fusion.1), channel_id=1, source_target_pairs={{1,0},{2,1},{3,2},{4,3},{5,4},{6,5},{7,6},{8,7},{9,8},{10,9},{11,1... | collective-permute-start | bytes 1572872 | tf_op jit(solution)/shard_map/ppermute | solution.py:264
  148.8 42.2 %copy-start.5 = (f32[4,384,384]{2,1,0:T(8,128)S(1)}, f32[4,384,384]{2,1,0:T(8,128)}, u32[]{:S(2)}) copy-start(f32[4,384,384]{2,1,0:T(8,128)} %get-tuple-element.36) | copy-start | bytes 7077892
  148.9 7.2 %collective-permute-start.18 = (f32[2,4,32,128]{3,2,1,0:T(8,128)S(1)}, f32[2,4,32,128]{3,2,1,0:T(8,128)S(1)}, u32[]{:S(2)}, u32[]{:S(2)}) collective-permute-start(f32[2,4,32,128]{3,2,1,0:T(8,128)S(1)} %slice.151), channel_id=1, source_target_pairs={{0,48},{16,0},{32,16},{48,32},{64,112},{80,64},{96,80},{112,96},{1... | collective-permute-start | bytes 393224 | tf_op jit(solution)/shard_map/ppermute | solution.py:257
  150.0 18.6 %collective-permute-start.15 = (f32[4,128,128]{2,1,0:T(8,128)S(1)}, f32[4,128,128]{2,1,0:T(8,128)S(1)}, u32[]{:S(2)}, u32[]{:S(2)}) collective-permute-start(f32[4,128,128]{2,1,0:T(8,128)S(1)} %slice_bitcast_fusion.8), channel_id=1, source_target_pairs={{0,1},{1,2},{2,3},{3,4},{4,5},{5,6},{6,7},{7,8},{8,9},{9,10},{10,1... | collective-permute-start | bytes 786440 | tf_op jit(solution)/shard_map/ppermute | solution.py:264
  152.0 23.1 %collective-permute-start.17 = (f32[2,4,96,128]{3,2,1,0:T(8,128)S(1)}, f32[2,4,96,128]{3,2,1,0:T(8,128)S(1)}, u32[]{:S(2)}, u32[]{:S(2)}) collective-permute-start(f32[2,4,96,128]{3,2,1,0:T(8,128)S(1)} %slice.150), channel_id=1, source_target_pairs={{0,16},{16,32},{32,48},{48,64},{64,80},{80,96},{96,112},{112,128},... | collective-permute-start | bytes 1179656 | tf_op jit(solution)/shard_map/ppermute | solution.py:264
  156.1 7.4 %collective-permute-start.19 = (f32[2,4,32,128]{3,2,1,0:T(8,128)S(1)}, f32[2,4,32,128]{3,2,1,0:T(8,128)S(1)}, u32[]{:S(2)}, u32[]{:S(2)}) collective-permute-start(f32[2,4,32,128]{3,2,1,0:T(8,128)S(1)} %collective-permute-done.18), channel_id=1, source_target_pairs={{0,48},{16,0},{32,16},{48,32},{64,112},{80,64},{96,80},{112,96},{1... | collective-permute-start | bytes 393224 | tf_op jit(solution)/shard_map/ppermute | solution.py:257
  160.1 31.1 %collective-permute-start.21 = (f32[3,4,128,128]{3,2,1,0:T(8,128)S(1)}, f32[3,4,128,128]{3,2,1,0:T(8,128)S(1)}, u32[]{:S(2)}, u32[]{:S(2)}) collective-permute-start(f32[3,4,128,128]{3,2,1,0:T(8,128)S(1)} %slice.155), channel_id=1, source_target_pairs={{0,1},{1,2},{2,3},{3,4},{4,5},{5,6},{6,7},{7,8},{8,9},{9,10},{10,1... | collective-permute-start | bytes 2359304 | tf_op jit(solution)/shard_map/ppermute | solution.py:264
  163.5 11.7 %collective-permute-start.20 = (f32[2,4,32,128]{3,2,1,0:T(8,128)S(1)}, f32[2,4,32,128]{3,2,1,0:T(8,128)S(1)}, u32[]{:S(2)}, u32[]{:S(2)}) collective-permute-start(f32[2,4,32,128]{3,2,1,0:T(8,128)S(1)} %collective-permute-done.19), channel_id=1, source_target_pairs={{0,48},{16,64},{32,16},{48,32},{64,112},{80,128},{96,80},{112,96},... | collective-permute-start | bytes 393224 | tf_op jit(solution)/shard_map/ppermute | solution.py:257
  168.6 22.4 %collective-permute-start.16 = (f32[4,128,128]{2,1,0:T(8,128)S(1)}, f32[4,128,128]{2,1,0:T(8,128)S(1)}, u32[]{:S(2)}, u32[]{:S(2)}) collective-permute-start(f32[4,128,128]{2,1,0:T(8,128)S(1)} %bitcast_add_fusion), channel_id=1, source_target_pairs={{0,16},{16,32},{32,48},{48,64},{64,80},{80,96},{96,112},{112,128},... | collective-permute-start | bytes 786440 | tf_op jit(solution)/shard_map/ppermute | solution.py:264
  191.5 1.4 copy-start.6

commit v3 on v2

--- a/solution.py
+++ b/solution.py
@@ -13,7 +13,7 @@
 STEP = 0.2
 B = 128
 ROWS, RING = 16, 4
-SHARE = 32
+SHARE = 24
 GROUP = 8
 
 

time: 197 us -> 204 us (1.036)
  the two profiles are of different devices: /device:TPU:23 before, /device:TPU:29 now
where the time goes in v3:
time: 204 us; the launch traced here: 203 us
  starting transfers between devices  85.1 us (42%)
  waiting for transfers between devices  71.4 us (35%)
  Pallas kernels  31.3 us (15%)
  local copies, waits for them, and re-layouts  11.9 us (6%)
  other arithmetic  2.83 us (1%)
    ppermute x16, starting transfers between devices, passed_along(): return lax.ppermute(x, axis, pairs)  71 us
    ppermute x16, waiting for transfers between devices, passed_along(): return lax.ppermute(x, axis, pairs)  65 us
    pallas_call x2, Pallas kernels, frame_grads(): pl.pallas_call(functools.partial(frames_kernel, last, len(pieces)), out_s...  31.3 us
    ppermute x6, starting transfers between devices, passed_around(): x = lax.ppermute(x, 'row', pairs)  14.1 us
    ppermute x6, waiting for transfers between devices, passed_around(): x = lax.ppermute(x, 'row', pairs)  6.44 us
  transfers between devices with their start and end apart: 22, of which 8 were waited for; matrix products, arithmetic and copies ran while one was open for 5% of the time, Pallas kernels for 0%

profile of v3, /device:TPU:29, one launch (start us, length us, event | category | flops | bytes accessed | tf_op | source)
XLA Modules:
  0.0 203.1 jit_solution(17875535026520249521)
XLA Ops:
  0.0 2.2 %slice.156 = f32[4,384,128]{2,1,0:T(8,128)} slice(f32[4,384,384]{2,1,0:T(8,128)} %bitcast.71), slice={[0:4], [0:384], [0:128]} | slice | bytes 1572864 | tf_op jit(solution)/shard_map/slice | solution.py:278
  2.2 2.6 %collective-permute-start = (f32[4,384,128]{2,1,0:T(8,128)}, f32[4,384,128]{2,1,0:T(8,128)S(1)}, u32[]{:S(2)}, u32[]{:S(2)}) collective-permute-start(f32[4,384,128]{2,1,0:T(8,128)} %slice.156), channel_id=1, source_target_pairs={{1,0},{2,1},{3,2},{4,3},{5,4},{6,5},{7,6},{8,7},{9,8},{10,9},{11,1... | collective-permute-start | bytes 2359304 | tf_op jit(solution)/shard_map/ppermute | solution.py:264
  5.8 8.1 %collective-permute-start.1 = (f32[4,128,128]{2,1,0:T(8,128)S(1)}, f32[4,128,128]{2,1,0:T(8,128)S(1)}, u32[]{:S(2)}, u32[]{:S(2)}) collective-permute-start(f32[4,128,128]{2,1,0:T(8,128)S(1)} %slice.157), channel_id=1, source_target_pairs={{16,0},{32,16},{48,32},{64,48},{80,64},{96,80},{112,96},{128,112},... | collective-permute-start | bytes 786440 | tf_op jit(solution)/shard_map/ppermute | solution.py:264
  15.9 5.4 %collective-permute-start.2 = (f32[4,104,256]{2,1,0:T(8,128)S(1)}, f32[4,104,256]{2,1,0:T(8,128)S(1)}, u32[]{:S(2)}, u32[]{:S(2)}) collective-permute-start(f32[4,104,256]{2,1,0:T(8,128)S(1)} %slice.158), channel_id=1, source_target_pairs={{16,0},{32,16},{48,32},{64,48},{80,64},{96,80},{112,96},{128,112},... | collective-permute-start | bytes 1277960 | tf_op jit(solution)/shard_map/ppermute | solution.py:264
  21.2 1.8 collective-permute-done.3
  23.0 6.0 %collective-permute-start.6 = (f32[4,128,128]{2,1,0:T(8,128)S(1)}, f32[4,128,128]{2,1,0:T(8,128)S(1)}, u32[]{:S(2)}, u32[]{:S(2)}) collective-permute-start(f32[4,128,128]{2,1,0:T(8,128)S(1)} %collective-permute-done.1.refs_2_), channel_id=1, source_target_pairs={{1,0},{2,1},{3,2},{4,3},{5,4},{6,5},{7,6},{8,7},{9,8},{10,9},{11,1... | collective-permute-start | bytes 786440 | tf_op jit(solution)/shard_map/ppermute | solution.py:264
  30.5 2.5 %collective-permute-start.5 = (f32[4,24,256]{2,1,0:T(8,128)}, f32[4,24,256]{2,1,0:T(8,128)S(1)}, u32[]{:S(2)}, u32[]{:S(2)}) collective-permute-start(f32[4,24,256]{2,1,0:T(8,128)} %collective-permute-done.4), channel_id=1, source_target_pairs={{0,16},{16,32},{48,0},{64,80},{80,96},{96,48},{112,64},{128,144},{... | collective-permute-start | bytes 294920 | tf_op jit(solution)/shard_map/ppermute | solution.py:257
  33.9 4.3 %collective-permute-done.5.refs_4_ = f32[4,24,256]{2,1,0:T(8,128)S(1)} collective-permute-done((f32[4,24,256]{2,1,0:T(8,128)}, f32[4,24,256]{2,1,0:T(8,128)S(1)}, u32[]{:S(2)}, u32[]{:S(2)}) %collective-permute-start.5) | collective-permute-done | bytes 98336 | tf_op jit(solution)/shard_map/ppermute | solution.py:257
  38.2 12.4 %collective-permute-done.6.refs_5_ = f32[4,128,128]{2,1,0:T(8,128)S(1)} collective-permute-done((f32[4,128,128]{2,1,0:T(8,128)S(1)}, f32[4,128,128]{2,1,0:T(8,128)S(1)}, u32[]{:S(2)}, u32[]{:S(2)}) %collective-permute-start.6) | collective-permute-done | bytes 262176 | tf_op jit(solution)/shard_map/ppermute | solution.py:264
  50.6 16.9 %frames.1 = (f32[4,4,4,128,128]{4,3,2,1,0:T(8,128)}, f32[4,3,4,128,128]{4,3,2,1,0:T(8,128)}) custom-call(s32[8,2]{1,0:T(8,128)S(1)} %copy.15.pos_ref, s32[1]{0:T(128)} %bitcast.cnt_ref, f32[4,384,384]{2,1,0:T(8,128)} %bitcast.75, f32[4,384,128]{2,1,0:T(8,128)S(1)} %collective-permute-done.refs_1_, f32[4,128,128]{2,1,0:T(8,128)S(1)} %collective-permute-done.1.refs_2_, ...), custom_call_target="tpu_custom_call" | custom-call | flops 2000000000 | bytes 9000000 | tf_op jit(solution)/shard_map/frames/pallas_call | solution.py:226
  68.7 8.1 %collective-permute-start.9 = (f32[2,4,128,128]{3,2,1,0:T(8,128)S(1)}, f32[2,4,128,128]{3,2,1,0:T(8,128)S(1)}, u32[]{:S(2)}, u32[]{:S(2)}) collective-permute-start(f32[2,4,128,128]{3,2,1,0:T(8,128)S(1)} %pad_maximum_fusion), channel_id=1, source_target_pairs={{0,1},{1,2},{2,3},{3,4},{4,5},{5,6},{6,7},{7,8},{8,9},{9,10},{10,1... | collective-permute-start | bytes 1572872 | tf_op jit(solution)/shard_map/ppermute | solution.py:264
  77.9 1.9 collective-permute-start.8
  79.8 1.4 slice_bitcast_fusion.2
  81.3 4.4 %collective-permute-start.12 = (f32[2,4,128,128]{3,2,1,0:T(8,128)S(1)}, f32[2,4,128,128]{3,2,1,0:T(8,128)S(1)}, u32[]{:S(2)}, u32[]{:S(2)}) collective-permute-start(f32[2,4,128,128]{3,2,1,0:T(8,128)S(1)} %get-tuple-element.41), channel_id=1, source_target_pairs={{16,0},{32,16},{48,32},{64,48},{80,64},{96,80},{112,96},{128,112},... | collective-permute-start | bytes 1572872 | tf_op jit(solution)/shard_map/ppermute | solution.py:264
  85.7 2.7 %collective-permute-start.7 = (f32[2,4,128,128]{3,2,1,0:T(8,128)S(1)}, f32[2,4,128,128]{3,2,1,0:T(8,128)S(1)}, u32[]{:S(2)}, u32[]{:S(2)}) collective-permute-start(f32[2,4,128,128]{3,2,1,0:T(8,128)S(1)} %get-tuple-element.42), channel_id=1, source_target_pairs={{0,16},{16,32},{32,48},{48,64},{64,80},{80,96},{96,112},{112,128},... | collective-permute-start | bytes 1572872 | tf_op jit(solution)/shard_map/ppermute | solution.py:264
  89.5 5.6 %collective-permute-start.13 = (f32[4,128,128]{2,1,0:T(8,128)S(1)}, f32[4,128,128]{2,1,0:T(8,128)S(1)}, u32[]{:S(2)}, u32[]{:S(2)}) collective-permute-start(f32[4,128,128]{2,1,0:T(8,128)S(1)} %get-tuple-element.39), channel_id=1, source_target_pairs={{16,0},{32,16},{48,32},{64,48},{80,64},{96,80},{112,96},{128,112},... | collective-permute-start | bytes 786440 | tf_op jit(solution)/shard_map/ppermute | solution.py:264
  95.1 1.9 collective-permute-start.10
  97.1 11.8 %collective-permute-start.11 = (f32[2,4,128,128]{3,2,1,0:T(8,128)S(1)}, f32[2,4,128,128]{3,2,1,0:T(8,128)S(1)}, u32[]{:S(2)}, u32[]{:S(2)}) collective-permute-start(f32[2,4,128,128]{3,2,1,0:T(8,128)S(1)} %fusion.3.refs_2_), channel_id=1, source_target_pairs={{1,0},{2,1},{3,2},{4,3},{5,4},{6,5},{7,6},{8,7},{9,8},{10,9},{11,1... | collective-permute-start | bytes 1572872 | tf_op jit(solution)/shard_map/ppermute | solution.py:264
  108.9 16.4 %collective-permute-done.10 = f32[4,128,128]{2,1,0:T(8,128)S(1)} collective-permute-done((f32[4,128,128]{2,1,0:T(8,128)S(1)}, f32[4,128,128]{2,1,0:T(8,128)S(1)}, u32[]{:S(2)}, u32[]{:S(2)}) %collective-permute-start.10) | collective-permute-done | bytes 262176 | tf_op jit(solution)/shard_map/ppermute | solution.py:264
  125.4 2.5 %collective-permute-start.14 = (f32[2,4,128,128]{3,2,1,0:T(8,128)S(1)}, f32[2,4,128,128]{3,2,1,0:T(8,128)S(1)}, u32[]{:S(2)}, u32[]{:S(2)}) collective-permute-start(f32[2,4,128,128]{3,2,1,0:T(8,128)S(1)} %pad_maximum_fusion.1), channel_id=1, source_target_pairs={{1,0},{2,1},{3,2},{4,3},{5,4},{6,5},{7,6},{8,7},{9,8},{10,9},{11,1... | collective-permute-start | bytes 1572872 | tf_op jit(solution)/shard_map/ppermute | solution.py:264
  128.1 7.8 %collective-permute-done.14.refs_7_ = f32[2,4,128,128]{3,2,1,0:T(8,128)S(1)} collective-permute-done((f32[2,4,128,128]{3,2,1,0:T(8,128)S(1)}, f32[2,4,128,128]{3,2,1,0:T(8,128)S(1)}, u32[]{:S(2)}, u32[]{:S(2)}) %collective-permute-start.14) | collective-permute-done | bytes 524320 | tf_op jit(solution)/shard_map/ppermute | solution.py:264
  135.9 14.4 %last_frames.1 = (f32[4,384,384]{2,1,0:T(8,128)}, f32[4,4,128,128]{3,2,1,0:T(8,128)S(1)}, f32[3,4,128,128]{3,2,1,0:T(8,128)S(1)}) custom-call(s32[8,2]{1,0:T(8,128)S(1)} %copy.15.pos_ref, s32[1]{0:T(128)} %bitcast.cnt_ref, f32[4,4,128,128]{3,2,1,0:T(8,128)S(1)} %bitcast.69, f32[2,4,128,128]{3,2,1,0:T(8,128)S(1)} %get-tuple-element.48.refs_1_, ...), custom_call_target="tpu_custom_call" | custom-call | flops 2000000000 | bytes 9000000 | tf_op jit(solution)/shard_map/last_frames/pallas_call | solution.py:226
  150.4 2.1 %collective-permute-start.15 = (f32[4,128,128]{2,1,0:T(8,128)S(1)}, f32[4,128,128]{2,1,0:T(8,128)S(1)}, u32[]{:S(2)}, u32[]{:S(2)}) collective-permute-start(f32[4,128,128]{2,1,0:T(8,128)S(1)} %slice_bitcast_fusion.8), channel_id=1, source_target_pairs={{0,1},{1,2},{2,3},{3,4},{4,5},{5,6},{6,7},{7,8},{8,9},{9,10},{10,1... | collective-permute-start | bytes 786440 | tf_op jit(solution)/shard_map/ppermute | solution.py:264
  152.4 3.9 %collective-permute-start.18 = (f32[2,4,24,128]{3,2,1,0:T(8,128)S(1)}, f32[2,4,24,128]{3,2,1,0:T(8,128)S(1)}, u32[]{:S(2)}, u32[]{:S(2)}) collective-permute-start(f32[2,4,24,128]{3,2,1,0:T(8,128)S(1)} %slice.151), channel_id=1, source_target_pairs={{0,48},{16,0},{32,16},{48,32},{64,112},{80,64},{96,80},{112,96},{1... | collective-permute-start | bytes 294920 | tf_op jit(solution)/shard_map/ppermute | solution.py:257
  156.4 1.9 collective-permute-start.17
  158.7 4.5 %collective-permute-start.19 = (f32[2,4,24,128]{3,2,1,0:T(8,128)S(1)}, f32[2,4,24,128]{3,2,1,0:T(8,128)S(1)}, u32[]{:S(2)}, u32[]{:S(2)}) collective-permute-start(f32[2,4,24,128]{3,2,1,0:T(8,128)S(1)} %collective-permute-done.18), channel_id=1, source_target_pairs={{0,48},{16,0},{32,16},{48,32},{64,112},{80,64},{96,80},{112,96},{1... | collective-permute-start | bytes 294920 | tf_op jit(solution)/shard_map/ppermute | solution.py:257
  163.3 4.2 %collective-permute-start.21 = (f32[3,4,128,128]{3,2,1,0:T(8,128)S(1)}, f32[3,4,128,128]{3,2,1,0:T(8,128)S(1)}, u32[]{:S(2)}, u32[]{:S(2)}) collective-permute-start(f32[3,4,128,128]{3,2,1,0:T(8,128)S(1)} %slice.155), channel_id=1, source_target_pairs={{0,1},{1,2},{2,3},{3,4},{4,5},{5,6},{6,7},{7,8},{8,9},{9,10},{10,1... | collective-permute-start | bytes 2359304 | tf_op jit(solution)/shard_map/ppermute | solution.py:264
  167.5 3.2 %collective-permute-start.20 = (f32[2,4,24,128]{3,2,1,0:T(8,128)S(1)}, f32[2,4,24,128]{3,2,1,0:T(8,128)S(1)}, u32[]{:S(2)}, u32[]{:S(2)}) collective-permute-start(f32[2,4,24,128]{3,2,1,0:T(8,128)S(1)} %collective-permute-done.19), channel_id=1, source_target_pairs={{0,48},{16,64},{32,16},{48,32},{64,112},{80,128},{96,80},{112,96},... | collective-permute-start | bytes 294920 | tf_op jit(solution)/shard_map/ppermute | solution.py:257
  170.8 1.9 collective-permute-start.16
  172.7 8.2 %collective-permute-done.17 = f32[2,4,104,128]{3,2,1,0:T(8,128)S(1)} collective-permute-done((f32[2,4,104,128]{3,2,1,0:T(8,128)S(1)}, f32[2,4,104,128]{3,2,1,0:T(8,128)S(1)}, u32[]{:S(2)}, u32[]{:S(2)}) %collective-permute-start.17) | collective-permute-done | bytes 426016 | tf_op jit(solution)/shard_map/ppermute | solution.py:264
  181.1 20.1 %collective-permute-done.16 = f32[4,128,128]{2,1,0:T(8,128)S(1)} collective-permute-done((f32[4,128,128]{2,1,0:T(8,128)S(1)}, f32[4,128,128]{2,1,0:T(8,128)S(1)}, u32[]{:S(2)}, u32[]{:S(2)}) %collective-permute-start.16) | collective-permute-done | bytes 262176 | tf_op jit(solution)/shard_map/ppermute | solution.py:264
  201.7 1.4 copy-done.6
  (62 shorter events, 10.2 us)
Async XLA Ops:
  0.0 30.0 %copy-start = (s32[1,16]{1,0:T(1,128)S(1)}, s32[1,16]{1,0:T(1,128)}, u32[]{:S(2)}) copy-start(s32[1,16]{1,0:T(1,128)} %param.16) | copy-start | bytes 196
  0.0 50.6 %copy-start.3 = (bf16[4,256,256]{2,1,0:T(8,128)(2,1)S(1)}, bf16[4,256,256]{2,1,0:T(8,128)(2,1)}, u32[]{:S(2)}) copy-start(bf16[4,256,256]{2,1,0:T(8,128)(2,1)} %constant.72.clone.refs_9_.refs_11_) | copy-start | bytes 1572868
  0.0 29.0 %copy-start.7 = (f32[128,128]{1,0:T(8,128)S(1)}, f32[128,128]{1,0:T(8,128)}, u32[]{:S(2)}) copy-start(f32[128,128]{1,0:T(8,128)} %param.13) | copy-start | bytes 196612
  0.0 29.9 %copy-start.8 = (s32[8,2]{0,1:T(2,128)S(1)}, s32[8,2]{0,1:T(2,128)}, u32[]{:S(2)}) copy-start(s32[8,2]{0,1:T(2,128)} %param.15) | copy-start | bytes 196
  0.0 50.6 %copy-start.1 = (f32[8,128,128]{2,1,0:T(8,128)S(1)}, f32[8,128,128]{2,1,0:T(8,128)}, u32[]{:S(2)}) copy-start(f32[8,128,128]{2,1,0:T(8,128)} %refs_8_.1) | copy-start | bytes 1572868
  0.0 50.6 %copy-start.2 = (f32[2,128,128]{2,1,0:T(8,128)S(1)}, f32[2,128,128]{2,1,0:T(8,128)}, u32[]{:S(2)}) copy-start(f32[2,128,128]{2,1,0:T(8,128)} %refs_9_.2) | copy-start | bytes 393220
  2.2 48.4 %collective-permute-start = (f32[4,384,128]{2,1,0:T(8,128)}, f32[4,384,128]{2,1,0:T(8,128)S(1)}, u32[]{:S(2)}, u32[]{:S(2)}) collective-permute-start(f32[4,384,128]{2,1,0:T(8,128)} %slice.156), channel_id=1, source_target_pairs={{1,0},{2,1},{3,2},{4,3},{5,4},{6,5},{7,6},{8,7},{9,8},{10,9},{11,1... | collective-permute-start | bytes 2359304 | tf_op jit(solution)/shard_map/ppermute | solution.py:264
  5.8 17.2 %collective-permute-start.1 = (f32[4,128,128]{2,1,0:T(8,128)S(1)}, f32[4,128,128]{2,1,0:T(8,128)S(1)}, u32[]{:S(2)}, u32[]{:S(2)}) collective-permute-start(f32[4,128,128]{2,1,0:T(8,128)S(1)} %slice.157), channel_id=1, source_target_pairs={{16,0},{32,16},{48,32},{64,48},{80,64},{96,80},{112,96},{128,112},... | collective-permute-start | bytes 786440 | tf_op jit(solution)/shard_map/ppermute | solution.py:264
  14.8 8.2 %collective-permute-start.3 = (f32[4,24,256]{2,1,0:T(8,128)S(1)}, f32[4,24,256]{2,1,0:T(8,128)}, u32[]{:S(2)}, u32[]{:S(2)}) collective-permute-start(f32[4,24,256]{2,1,0:T(8,128)S(1)} %slice.159), channel_id=1, source_target_pairs={{0,16},{16,32},{32,48},{48,0},{64,80},{80,96},{96,112},{112,64},{1... | collective-permute-start | bytes 294920 | tf_op jit(solution)/shard_map/ppermute | solution.py:257
  15.9 22.3 %collective-permute-start.2 = (f32[4,104,256]{2,1,0:T(8,128)S(1)}, f32[4,104,256]{2,1,0:T(8,128)S(1)}, u32[]{:S(2)}, u32[]{:S(2)}) collective-permute-start(f32[4,104,256]{2,1,0:T(8,128)S(1)} %slice.158), channel_id=1, source_target_pairs={{16,0},{32,16},{48,32},{64,48},{80,64},{96,80},{112,96},{128,112},... | collective-permute-start | bytes 1277960 | tf_op jit(solution)/shard_map/ppermute | solution.py:264
  23.0 7.6 %collective-permute-start.4 = (f32[4,24,256]{2,1,0:T(8,128)}, f32[4,24,256]{2,1,0:T(8,128)}, u32[]{:S(2)}, u32[]{:S(2)}) collective-permute-start(f32[4,24,256]{2,1,0:T(8,128)} %collective-permute-done.3), channel_id=1, source_target_pairs={{0,16},{16,32},{32,48},{48,0},{64,80},{80,96},{96,112},{112,64},{1... | collective-permute-start | bytes 294920 | tf_op jit(solution)/shard_map/ppermute | solution.py:257
  23.0 27.6 %collective-permute-start.6 = (f32[4,128,128]{2,1,0:T(8,128)S(1)}, f32[4,128,128]{2,1,0:T(8,128)S(1)}, u32[]{:S(2)}, u32[]{:S(2)}) collective-permute-start(f32[4,128,128]{2,1,0:T(8,128)S(1)} %collective-permute-done.1.refs_2_), channel_id=1, source_target_pairs={{1,0},{2,1},{3,2},{4,3},{5,4},{6,5},{7,6},{8,7},{9,8},{10,9},{11,1... | collective-permute-start | bytes 786440 | tf_op jit(solution)/shard_map/ppermute | solution.py:264
  30.5 7.7 %collective-permute-start.5 = (f32[4,24,256]{2,1,0:T(8,128)}, f32[4,24,256]{2,1,0:T(8,128)S(1)}, u32[]{:S(2)}, u32[]{:S(2)}) collective-permute-start(f32[4,24,256]{2,1,0:T(8,128)} %collective-permute-done.4), channel_id=1, source_target_pairs={{0,16},{16,32},{48,0},{64,80},{80,96},{96,48},{112,64},{128,144},{... | collective-permute-start | bytes 294920 | tf_op jit(solution)/shard_map/ppermute | solution.py:257
  68.7 19.7 %collective-permute-start.9 = (f32[2,4,128,128]{3,2,1,0:T(8,128)S(1)}, f32[2,4,128,128]{3,2,1,0:T(8,128)S(1)}, u32[]{:S(2)}, u32[]{:S(2)}) collective-permute-start(f32[2,4,128,128]{3,2,1,0:T(8,128)S(1)} %pad_maximum_fusion), channel_id=1, source_target_pairs={{0,1},{1,2},{2,3},{3,4},{4,5},{5,6},{6,7},{7,8},{8,9},{9,10},{10,1... | collective-permute-start | bytes 1572872 | tf_op jit(solution)/shard_map/ppermute | solution.py:264
  77.9 19.2 %collective-permute-start.8 = (f32[2,4,128,128]{3,2,1,0:T(8,128)S(1)}, f32[2,4,128,128]{3,2,1,0:T(8,128)S(1)}, u32[]{:S(2)}, u32[]{:S(2)}) collective-permute-start(f32[2,4,128,128]{3,2,1,0:T(8,128)S(1)} %slice_bitcast_fusion), channel_id=1, source_target_pairs={{0,1},{1,2},{2,3},{3,4},{4,5},{5,6},{6,7},{7,8},{8,9},{9,10},{10,1... | collective-permute-start | bytes 1572872 | tf_op jit(solution)/shard_map/ppermute | solution.py:264
  79.8 17.3 %copy-start.4 = (f32[4,3,4,128,128]{4,3,2,1,0:T(8,128)S(1)}, f32[4,3,4,128,128]{4,3,2,1,0:T(8,128)}, u32[]{:S(2)}) copy-start(f32[4,3,4,128,128]{4,3,2,1,0:T(8,128)} %get-tuple-element.34) | copy-start | bytes 9437188
  81.3 46.7 %collective-permute-start.12 = (f32[2,4,128,128]{3,2,1,0:T(8,128)S(1)}, f32[2,4,128,128]{3,2,1,0:T(8,128)S(1)}, u32[]{:S(2)}, u32[]{:S(2)}) collective-permute-start(f32[2,4,128,128]{3,2,1,0:T(8,128)S(1)} %get-tuple-element.41), channel_id=1, source_target_pairs={{16,0},{32,16},{48,32},{64,48},{80,64},{96,80},{112,96},{128,112},... | collective-permute-start | bytes 1572872 | tf_op jit(solution)/shard_map/ppermute | solution.py:264
  85.7 42.3 %collective-permute-start.7 = (f32[2,4,128,128]{3,2,1,0:T(8,128)S(1)}, f32[2,4,128,128]{3,2,1,0:T(8,128)S(1)}, u32[]{:S(2)}, u32[]{:S(2)}) collective-permute-start(f32[2,4,128,128]{3,2,1,0:T(8,128)S(1)} %get-tuple-element.42), channel_id=1, source_target_pairs={{0,16},{16,32},{32,48},{48,64},{64,80},{80,96},{96,112},{112,128},... | collective-permute-start | bytes 1572872 | tf_op jit(solution)/shard_map/ppermute | solution.py:264
  89.5 19.4 %collective-permute-start.13 = (f32[4,128,128]{2,1,0:T(8,128)S(1)}, f32[4,128,128]{2,1,0:T(8,128)S(1)}, u32[]{:S(2)}, u32[]{:S(2)}) collective-permute-start(f32[4,128,128]{2,1,0:T(8,128)S(1)} %get-tuple-element.39), channel_id=1, source_target_pairs={{16,0},{32,16},{48,32},{64,48},{80,64},{96,80},{112,96},{128,112},... | collective-permute-start | bytes 786440 | tf_op jit(solution)/shard_map/ppermute | solution.py:264
  95.1 30.2 %collective-permute-start.10 = (f32[4,128,128]{2,1,0:T(8,128)S(1)}, f32[4,128,128]{2,1,0:T(8,128)S(1)}, u32[]{:S(2)}, u32[]{:S(2)}) collective-permute-start(f32[4,128,128]{2,1,0:T(8,128)S(1)} %get-tuple-element.40), channel_id=1, source_target_pairs={{0,16},{16,32},{32,48},{48,64},{64,80},{80,96},{96,112},{112,128},... | collective-permute-start | bytes 786440 | tf_op jit(solution)/shard_map/ppermute | solution.py:264
  97.1 31.0 %collective-permute-start.11 = (f32[2,4,128,128]{3,2,1,0:T(8,128)S(1)}, f32[2,4,128,128]{3,2,1,0:T(8,128)S(1)}, u32[]{:S(2)}, u32[]{:S(2)}) collective-permute-start(f32[2,4,128,128]{3,2,1,0:T(8,128)S(1)} %fusion.3.refs_2_), channel_id=1, source_target_pairs={{1,0},{2,1},{3,2},{4,3},{5,4},{6,5},{7,6},{8,7},{9,8},{10,9},{11,1... | collective-permute-start | bytes 1572872 | tf_op jit(solution)/shard_map/ppermute | solution.py:264
  125.4 10.5 %collective-permute-start.14 = (f32[2,4,128,128]{3,2,1,0:T(8,128)S(1)}, f32[2,4,128,128]{3,2,1,0:T(8,128)S(1)}, u32[]{:S(2)}, u32[]{:S(2)}) collective-permute-start(f32[2,4,128,128]{3,2,1,0:T(8,128)S(1)} %pad_maximum_fusion.1), channel_id=1, source_target_pairs={{1,0},{2,1},{3,2},{4,3},{5,4},{6,5},{7,6},{8,7},{9,8},{10,9},{11,1... | collective-permute-start | bytes 1572872 | tf_op jit(solution)/shard_map/ppermute | solution.py:264
  150.3 50.9 %copy-start.5 = (f32[4,384,384]{2,1,0:T(8,128)S(1)}, f32[4,384,384]{2,1,0:T(8,128)}, u32[]{:S(2)}) copy-start(f32[4,384,384]{2,1,0:T(8,128)} %get-tuple-element.36) | copy-start | bytes 7077892
  150.4 20.4 %collective-permute-start.15 = (f32[4,128,128]{2,1,0:T(8,128)S(1)}, f32[4,128,128]{2,1,0:T(8,128)S(1)}, u32[]{:S(2)}, u32[]{:S(2)}) collective-permute-start(f32[4,128,128]{2,1,0:T(8,128)S(1)} %slice_bitcast_fusion.8), channel_id=1, source_target_pairs={{0,1},{1,2},{2,3},{3,4},{4,5},{5,6},{6,7},{7,8},{8,9},{9,10},{10,1... | collective-permute-start | bytes 786440 | tf_op jit(solution)/shard_map/ppermute | solution.py:264
  152.4 6.2 %collective-permute-start.18 = (f32[2,4,24,128]{3,2,1,0:T(8,128)S(1)}, f32[2,4,24,128]{3,2,1,0:T(8,128)S(1)}, u32[]{:S(2)}, u32[]{:S(2)}) collective-permute-start(f32[2,4,24,128]{3,2,1,0:T(8,128)S(1)} %slice.151), channel_id=1, source_target_pairs={{0,48},{16,0},{32,16},{48,32},{64,112},{80,64},{96,80},{112,96},{1... | collective-permute-start | bytes 294920 | tf_op jit(solution)/shard_map/ppermute | solution.py:257
  156.4 24.6 %collective-permute-start.17 = (f32[2,4,104,128]{3,2,1,0:T(8,128)S(1)}, f32[2,4,104,128]{3,2,1,0:T(8,128)S(1)}, u32[]{:S(2)}, u32[]{:S(2)}) collective-permute-start(f32[2,4,104,128]{3,2,1,0:T(8,128)S(1)} %slice.150), channel_id=1, source_target_pairs={{0,16},{16,32},{32,48},{48,64},{64,80},{80,96},{96,112},{112,128},... | collective-permute-start | bytes 1277960 | tf_op jit(solution)/shard_map/ppermute | solution.py:264
  158.7 8.8 %collective-permute-start.19 = (f32[2,4,24,128]{3,2,1,0:T(8,128)S(1)}, f32[2,4,24,128]{3,2,1,0:T(8,128)S(1)}, u32[]{:S(2)}, u32[]{:S(2)}) collective-permute-start(f32[2,4,24,128]{3,2,1,0:T(8,128)S(1)} %collective-permute-done.18), channel_id=1, source_target_pairs={{0,48},{16,0},{32,16},{48,32},{64,112},{80,64},{96,80},{112,96},{1... | collective-permute-start | bytes 294920 | tf_op jit(solution)/shard_map/ppermute | solution.py:257
  163.3 38.1 %collective-permute-start.21 = (f32[3,4,128,128]{3,2,1,0:T(8,128)S(1)}, f32[3,4,128,128]{3,2,1,0:T(8,128)S(1)}, u32[]{:S(2)}, u32[]{:S(2)}) collective-permute-start(f32[3,4,128,128]{3,2,1,0:T(8,128)S(1)} %slice.155), channel_id=1, source_target_pairs={{0,1},{1,2},{2,3},{3,4},{4,5},{5,6},{6,7},{7,8},{8,9},{9,10},{10,1... | collective-permute-start | bytes 2359304 | tf_op jit(solution)/shard_map/ppermute | solution.py:264
  167.5 13.5 %collective-permute-start.20 = (f32[2,4,24,128]{3,2,1,0:T(8,128)S(1)}, f32[2,4,24,128]{3,2,1,0:T(8,128)S(1)}, u32[]{:S(2)}, u32[]{:S(2)}) collective-permute-start(f32[2,4,24,128]{3,2,1,0:T(8,128)S(1)} %collective-permute-done.19), channel_id=1, source_target_pairs={{0,48},{16,64},{32,16},{48,32},{64,112},{80,128},{96,80},{112,96},... | collective-permute-start | bytes 294920 | tf_op jit(solution)/shard_map/ppermute | solution.py:257
  170.8 30.4 %collective-permute-start.16 = (f32[4,128,128]{2,1,0:T(8,128)S(1)}, f32[4,128,128]{2,1,0:T(8,128)S(1)}, u32[]{:S(2)}, u32[]{:S(2)}) collective-permute-start(f32[4,128,128]{2,1,0:T(8,128)S(1)} %bitcast_add_fusion), channel_id=1, source_target_pairs={{0,16},{16,32},{32,48},{48,64},{64,80},{80,96},{96,112},{112,128},... | collective-permute-start | bytes 786440 | tf_op jit(solution)/shard_map/ppermute | solution.py:264
  201.7 1.4 copy-start.6
